TPU v7x, 512 devices: a whole 4x8x8 slice. The times are simulated.
512 devices in a mesh: ctx: 32 (over x, y), head: 16 (over z, core).
Axes of the slice: x: 4, y: 8, z: 8, core: 2. Of those that a mesh axis runs over, the one named last changes fastest.
Arguments:
- light_query: bfloat16 [65536, 2048], P(('ctx', 'head')), may hold values from -6 to 6
- light_key: bfloat16 [65536, 2048], P(('ctx', 'head')), may hold values from -6 to 6
- light_value: bfloat16 [65536, 2048], P(('ctx', 'head')), may hold values from -6 to 6
- soft_query: bfloat16 [65536, 2048], P(('ctx', 'head')), may hold values from -52 to 52
- soft_key: bfloat16 [65536, 2048], P(('ctx', 'head')), may hold values from -6 to 6
- upstream: bfloat16 [65536, 2048], P(('ctx', 'head')), may hold values from -6 to 6
- decays: bfloat16 [65536, 32], P(('ctx', 'head')), may hold values from 0 to 1
- block_mask: int32 [512, 16], P('ctx'), may hold values from 0 to 1, as said below
Outputs:
- grad_light_query: bfloat16 [65536, 2048], P(('ctx', 'head'))
- grad_light_key: bfloat16 [65536, 2048], P(('ctx', 'head'))
- grad_light_value: bfloat16 [65536, 2048], P(('ctx', 'head'))
Inputs may be any that keep to these rules, and one draw needn't show every extreme that they name: `block_mask`: in each query block, the flag of its own block within the span is 1 and flags of later blocks are 0; earlier blocks are 0 or 1.
All inputs are finite; a program needn't handle non-finite values.
Results may differ from a plain program's by a relative error of at most 0.0057.
Values may be sent and summed in bfloat16 or wider, within the bound.
A program may use at most 64 MiB of HBM per device.

v0:
```python
import math

import jax
import jax.numpy as jnp
from jax import lax
from jax.sharding import PartitionSpec as P

BLOCK = 128


HIGH = lax.Precision.HIGHEST


def prefix(shard, axis, combine, identity, reverse):
    peers, here = (lax.axis_size(axis), lax.axis_index(axis))
    everything = jax.tree.map(lambda part: lax.all_gather(part, axis), shard)
    start = jax.tree.map(
        lambda part, zero: jnp.broadcast_to(jnp.asarray(zero, part.dtype), part.shape),
        shard,
        identity,
    )

    def lap(k, before):
        at = peers - 1 - k if reverse else k
        reached = at > here if reverse else at < here
        new = combine(before, jax.tree.map(lambda part: part[at], everything))
        return jax.tree.map(lambda a, b: jnp.where(reached, a, b), new, before)

    return lax.fori_loop(0, peers, lap, start)


def combine_pairs(earlier, later):
    return (earlier[0] * later[0], later[0][:, None, None] * earlier[1] + later[1])


def span_tables(decay_rows):
    levels = jnp.cumsum(decay_rows.astype(jnp.float32).T, axis=1)
    count = levels.shape[1]
    places = jnp.arange(count)
    lower = places[None, :] <= places[:, None]
    spread = levels[:, None, :] - levels[:, :, None]
    weights = jnp.where(lower[None], jnp.exp(jnp.minimum(spread, 0.0)), 0.0)
    finals = levels[:, -1]
    entries = jnp.exp(-levels).T
    leaving = jnp.exp(levels - finals[:, None]).T
    return (weights, entries, leaving, jnp.exp(-finals))


def mixing(form, left, right):
    return jnp.einsum(form, left, right, preferred_element_type=jnp.float32)


def exact(form, left, right):
    return jnp.einsum(form, left, right, precision=HIGH)


def local_prefix(running_totals, sums, backward):
    identity = (jnp.ones_like(running_totals[0]), jnp.zeros_like(sums[0]))

    def carry_step(carried, item):
        return (combine_pairs(carried, item), carried)

    return lax.scan(carry_step, identity, (running_totals, sums), reverse=backward)


def body(light_query, light_key, light_value, soft_query, soft_key, upstream, decays, block_mask):
    query_one, key_one, value_one, query_two, key_two, cotan, decay_rows = (
        lax.all_to_all(light_query, "head", split_axis=1, concat_axis=0, tiled=True),
        lax.all_to_all(light_key, "head", split_axis=1, concat_axis=0, tiled=True),
        lax.all_to_all(light_value, "head", split_axis=1, concat_axis=0, tiled=True),
        lax.all_to_all(soft_query, "head", split_axis=1, concat_axis=0, tiled=True),
        lax.all_to_all(soft_key, "head", split_axis=1, concat_axis=0, tiled=True),
        lax.all_to_all(upstream, "head", split_axis=1, concat_axis=0, tiled=True),
        lax.all_to_all(decays, "head", split_axis=1, concat_axis=0, tiled=True),
    )
    length = query_one.shape[0]
    heads_here = decay_rows.shape[1]
    head_width = query_one.shape[1] // heads_here
    blocks = length // BLOCK
    scale = 1.0 / (head_width * math.sqrt(head_width))
    root = 1.0 / math.sqrt(head_width)

    def split_blocks(array):
        return array.reshape(blocks, BLOCK, heads_here, head_width)

    def join_heads(array):
        return array.reshape(length, heads_here * head_width)

    query_one = split_blocks(query_one)
    key_one = split_blocks(key_one)
    value_one = split_blocks(value_one)
    weights, entries, leaving, running_totals = jax.vmap(span_tables)(
        decay_rows.reshape(blocks, BLOCK, heads_here)
    )
    block_sums = exact(
        "nshi,nshj->nhij",
        key_one.astype(jnp.float32) * leaving[..., None],
        value_one.astype(jnp.float32),
    )
    whole, local_in = local_prefix(running_totals, block_sums, False)
    identity = (jnp.ones_like(running_totals[0]), jnp.zeros_like(block_sums[0]))
    device_in = prefix(whole, "ctx", combine_pairs, identity, False)
    state_in = local_in[0][:, :, None, None] * device_in[1][None] + local_in[1]
    query_two = query_two.reshape(length, heads_here, head_width)
    key_two = key_two.reshape(length, heads_here, head_width)
    cotan = cotan.reshape(length, heads_here, head_width)
    group = min(4 * BLOCK, length)
    group_blocks = group // BLOCK
    key_places = jnp.arange(length)
    summed = jnp.zeros((length, heads_here, head_width), jnp.float32)
    for number in range(length // group):
        first_row = number * group
        key_end = first_row + group
        query_group = query_two[first_row:key_end]
        cotan_group = cotan[first_row:key_end]
        flags = block_mask[number * group_blocks : (number + 1) * group_blocks, : key_end // BLOCK]
        open_pairs = jnp.repeat(jnp.repeat(flags, BLOCK, axis=0), BLOCK, axis=1) == 1
        query_places = first_row + jnp.arange(group)
        allowed = open_pairs & (key_places[None, :key_end] <= query_places[:, None])
        scores = mixing("thd,shd->hts", query_group, key_two[:key_end]) * root
        scores = jnp.where(allowed[None], scores, -jnp.inf)
        highest = jnp.max(scores, axis=-1, keepdims=True)
        powers = jnp.exp(scores - highest)
        probs = powers / jnp.sum(powers, axis=-1, keepdims=True)
        probs_low = probs.astype(jnp.bfloat16)
        summed = summed.at[:key_end].add(mixing("hts,thd->shd", probs_low, cotan_group))
    lit_grad = split_blocks(summed.astype(jnp.bfloat16))
    back = (mixing("nthd,nshd->nhts", lit_grad, value_one) * weights).astype(jnp.bfloat16)
    grad_q_one = scale * (
        mixing("nhts,nshd->nthd", back, key_one)
        + entries[..., None] * exact("nthj,nhij->nthi", lit_grad.astype(jnp.float32), state_in)
    )
    grad_q_one = join_heads(grad_q_one.astype(jnp.bfloat16))
    reach = exact(
        "nthi,nthj->nhij",
        query_one.astype(jnp.float32) * entries[..., None],
        lit_grad.astype(jnp.float32),
    )
    whole_reach, local_reach = local_prefix(running_totals, reach, True)
    device_reach = prefix(whole_reach, "ctx", combine_pairs, identity, True)
    reach_in = local_reach[0][:, :, None, None] * device_reach[1][None] + local_reach[1]
    mixed = (mixing("nthd,nshd->nhts", query_one, key_one) * weights).astype(jnp.bfloat16)
    grad_k_one = scale * (
        mixing("nhts,nthd->nshd", back, query_one)
        + leaving[..., None] * exact("nshj,nhij->nshi", value_one.astype(jnp.float32), reach_in)
    )
    grad_v_one = scale * (
        mixing("nhts,nthd->nshd", mixed, lit_grad)
        + leaving[..., None] * exact("nshi,nhij->nshj", key_one.astype(jnp.float32), reach_in)
    )
    grad_k_one = join_heads(grad_k_one.astype(jnp.bfloat16))
    grad_v_one = join_heads(grad_v_one.astype(jnp.bfloat16))
    light_query_grad, light_key_grad, light_value_grad = (
        lax.all_to_all(grad_q_one, "head", split_axis=0, concat_axis=1, tiled=True),
        lax.all_to_all(grad_k_one, "head", split_axis=0, concat_axis=1, tiled=True),
        lax.all_to_all(grad_v_one, "head", split_axis=0, concat_axis=1, tiled=True),
    )
    return (light_query_grad, light_key_grad, light_value_grad)


def solution(mesh):
    return jax.shard_map(
        body,
        mesh=mesh,
        in_specs=(
            P(("ctx", "head"), None),
            P(("ctx", "head"), None),
            P(("ctx", "head"), None),
            P(("ctx", "head"), None),
            P(("ctx", "head"), None),
            P(("ctx", "head"), None),
            P(("ctx", "head"), None),
            P("ctx", None),
        ),
        out_specs=(P(("ctx", "head"), None), P(("ctx", "head"), None), P(("ctx", "head"), None)),
        check_vma=False,
    )
```

profile of v0, /device:TPU:1, one launch (start us, length us, event | category | flops | bytes accessed | tf_op | source)
XLA Modules:
  0.0 446.2 jit_solution(16652031253214639902)
XLA Ops:
  7.2 11.8 %all-to-all-start.4 = ((bf16[128,16,2]{0,2,1:T(2,128)(2,1)}), bf16[128,16,2]{0,2,1:T(2,128)(2,1)S(1)}, u32[]{:S(2)}, u32[]{:S(2)}) async-start(bf16[128,16,2]{0,2,1:T(2,128)(2,1)} %bitcast.263), calls=%async_computation.4 | async-start | bytes 16384 | tf_op jit(solution)/shard_map/all_to_all | solution.py:74
  27.2 7.2 %all-to-all-start = ((bf16[128,16,128]{0,2,1:T(8,128)(2,1)}), bf16[128,16,128]{0,2,1:T(8,128)(2,1)S(1)}, u32[]{:S(2)}, u32[]{:S(2)}) async-start(bf16[128,16,128]{0,2,1:T(8,128)(2,1)} %bitcast.1), calls=%async_computation | async-start | bytes 1048576 | tf_op jit(solution)/shard_map/all_to_all | solution.py:71
  43.4 8.3 %all-to-all-done = bf16[128,16,128]{0,2,1:T(8,128)(2,1)S(1)} async-done(((bf16[128,16,128]{0,2,1:T(8,128)(2,1)}), bf16[128,16,128]{0,2,1:T(8,128)(2,1)S(1)}, u32[]{:S(2)}, u32[]{:S(2)}) %all-to-all-start) | async-done | bytes 524320 | tf_op jit(solution)/shard_map/all_to_all | solution.py:71
  51.7 3.5 all-to-all-start.1
  58.2 3.5 broadcast_in_dim.158
  62.8 9.1 %all-to-all-done.1 = bf16[128,16,128]{0,2,1:T(8,128)(2,1)S(1)} async-done(((bf16[128,16,128]{0,2,1:T(8,128)(2,1)}), bf16[128,16,128]{0,2,1:T(8,128)(2,1)S(1)}, u32[]{:S(2)}, u32[]{:S(2)}) %all-to-all-start.1) | async-done | bytes 524320 | tf_op jit(solution)/shard_map/all_to_all | solution.py:72
  71.9 3.5 all-to-all-start.2
  82.2 9.9 %all-to-all-done.2 = bf16[128,16,128]{0,2,1:T(8,128)(2,1)S(1)} async-done(((bf16[128,16,128]{0,2,1:T(8,128)(2,1)}), bf16[128,16,128]{0,2,1:T(8,128)(2,1)S(1)}, u32[]{:S(2)}, u32[]{:S(2)}) %all-to-all-start.2) | async-done | bytes 524320 | tf_op jit(solution)/shard_map/all_to_all | solution.py:73
  92.1 3.6 all-to-all-start.7
  104.8 2.5 fusion.114
  110.9 4.5 %fusion.115 = (f32[2,512]{1,0:T(2,128)S(1)}, f32[2,512,1024]{2,1,0:T(8,128)}) fusion(pred[512,1024]{1,0:T(8,128)(4,1)S(1)} %copy-done.9, bf16[512,2,64]{0,2,1:T(8,128)(2,1)} %slice.190, bf16[1024,2,64]{0,2,1:T(8,128)(2,1)S(1)} %copy-done.14), kind=kOutput, calls=%fused_computation.162 | convolution fusion | flops 138413056 | bytes 5115904 | tf_op jit(solution)/shard_map/sub | solution.py:123
  115.4 3.8 fusion.52
  119.2 3.9 fusion.116
  124.9 5.1 %fusion.26 = f32[2048,2,64]{0,2,1:T(8,128)} fusion(f32[2048,2,64]{0,2,1:T(8,128)} %fusion.52, bf16[512,2,64]{0,2,1:T(8,128)(2,1)} %slice.203, f32[2,512]{1,0:T(2,128)} %fusion.116, pred[512,1536]{1,0:T(8,128)(4,1)} %copy.71, bf16[512,2,64]{0,2,1:T(8,128)(2,1)S(1)} %copy-done.17, bf16[1536,2,64]{0,2,1:T(8,128)(2,1)} %slice.201), kind=kOutput, calls=%fused_computation.49 | convolution fusion | flops 410716672 | bytes 3018752 | tf_op jit(solution)/shard_map/hts,thd->shd/dot_general | solution.py:50
  130.0 5.0 %fusion.117 = (f32[2,512]{1,0:T(2,128)S(1)}, f32[2,512,2048]{2,1,0:T(8,128)}) fusion(pred[512,2048]{1,0:T(8,128)(4,1)S(1)} %fusion.16, bf16[512,2,64]{0,2,1:T(8,128)(2,1)S(1)} %slice.206, bf16[2048,2,64]{0,2,1:T(8,128)(2,1)S(1)} %reshape.376), kind=kOutput, calls=%fused_computation.164 | convolution fusion | flops 276826112 | bytes 10096640 | tf_op jit(solution)/shard_map/sub | solution.py:123
  135.0 6.5 %all-to-all-start.5 = ((bf16[128,16,128]{0,2,1:T(8,128)(2,1)}), bf16[128,16,128]{0,2,1:T(8,128)(2,1)S(1)}, u32[]{:S(2)}, u32[]{:S(2)}) async-start(bf16[128,16,128]{0,2,1:T(8,128)(2,1)} %bitcast.19), calls=%async_computation.5 | async-start | bytes 1048576 | tf_op jit(solution)/shard_map/all_to_all | solution.py:69
  141.6 4.6 %fusion.50 = bf16[2,8,16,8,128]{4,3,2,1,0:T(8,128)(2,1)S(1)} fusion(f32[2048,2,64]{0,2,1:T(8,128)} %fusion.26, bf16[512,2,64]{0,2,1:T(8,128)(2,1)S(1)} %slice.208, f32[2,512,2048]{2,1,0:T(8,128)} %get-tuple-element.674, f32[2,512]{1,0:T(2,128)S(1)} %get-tuple-element.673), kind=kOutput, calls=%fused_computation.85 | convolution fusion | flops 273154048 | bytes 10096640 | tf_op jit(solution)/shard_map/hts,thd->shd/dot_general | solution.py:50
  148.1 10.7 %all-to-all-done.5 = bf16[128,16,128]{0,2,1:T(8,128)(2,1)S(1)} async-done(((bf16[128,16,128]{0,2,1:T(8,128)(2,1)}), bf16[128,16,128]{0,2,1:T(8,128)(2,1)S(1)}, u32[]{:S(2)}, u32[]{:S(2)}) %all-to-all-start.5) | async-done | bytes 524320 | tf_op jit(solution)/shard_map/all_to_all | solution.py:69
  158.9 3.5 all-to-all-start.3
  162.5 26.7 %while.75 = (s32[]{:T(128)}, f32[2]{0:T(128)S(1)}, f32[2,64,64]{2,1,0:T(8,128)S(1)}, f32[16,2]{1,0:T(8,128)S(1)}, f32[16,2,64,64]{3,2,1,0:T(8,128)S(1)}, /*index...) while((s32[]{:T(128)}, f32[2]{0:T(128)S(1)}, ...), condition=%wide.region_14.15_spmd.clone, body=%wide.region_13.14_spmd.clone.sunk | while | flops 32776 | bytes 229581 | solution.py:63
  193.0 36.3 %while.73 = (s32[]{:T(128)}, f32[2]{0:T(128)S(1)}, f32[2,64,64]{2,1,0:T(8,128)S(1)}, f32[16,2]{1,0:T(8,128)S(1)}, f32[16,2,64,64]{3,2,1,0:T(8,128)}, /*index=5*/...) while((s32[]{:T(128)}, f32[2]{0:T(128)S(1)}, f32[2,64,64]{2,1,0:T(8,128)S(1)}, ...), condition=%wide.region_10.11_spmd.clone, body=%wide.region_9.10_spmd.clone.sunk | while | flops 32775 | bytes 197301 | solution.py:63
  229.8 61.9 %all-reduce.3 = (f32[64]{0:T(128)S(1)}, f32[64]{0:T(128)S(1)}) all-reduce(f32[64]{0:T(128)S(1)} %dynamic-update-slice.11, f32[64]{0:T(128)S(1)} %dynamic-update-slice.12), channel_id=2, replica_groups=mesh['ctx'=32,'head'=16] {'ctx'}, use_global_device_ids=true, to_apply=%add.1 | all-reduce | flops 128 | bytes 1024
  291.9 30.5 %while.76 = (s32[]{:T(128)}, f32[2,64,64]{2,1,0:T(8,128)S(1)}, s32[]{:T(128)}, f32[32,2]{1,0:T(8,128)S(1)}, f32[32,2,64,64]{3,2,1,0:T(8,128)}, /*index=5*/s32[]{:T(128)}, s32[]{:T(128)}, s32[]{:T(128)}, s32[]{:T(128)}) while((s32[]{:T(128)}, f32[2,64,64]{2,1,0:T(8,128)S(1)}, s32[]{:T(128)}, f32[32,2]{1,0:T(8,128)S(1)}, ...), condition=%wide.region_16.17_spmd.clone, body=%wide.region_15.16_spmd.clone.sunk | while | flops 32776 | bytes 98495 | solution.py:29
  324.5 3.1 fusion.46
  327.6 20.0 %all-to-all-start.9 = ((bf16[16,128,128]{1,2,0:T(8,128)(2,1)}), bf16[16,128,128]{1,2,0:T(8,128)(2,1)}, u32[]{:S(2)}, u32[]{:S(2)}) async-start(bf16[16,128,128]{1,2,0:T(8,128)(2,1)} %bitcast.255), calls=%async_computation.9 | async-start | bytes 1048576 | tf_op jit(solution)/shard_map/all_to_all | solution.py:156
  349.6 3.1 convolution_bitcast_fusion.4
  354.8 10.3 %all-to-all-done.9 = bf16[16,128,128]{1,2,0:T(8,128)(2,1)} async-done(((bf16[16,128,128]{1,2,0:T(8,128)(2,1)}), bf16[16,128,128]{1,2,0:T(8,128)(2,1)}, u32[]{:S(2)}, u32[]{:S(2)}) %all-to-all-start.9) | async-done | bytes 524320 | tf_op jit(solution)/shard_map/all_to_all | solution.py:156
  365.0 3.5 all-to-all-start.8
  368.5 9.0 %all-gather.7.cloned.1.call-done = f32[64,64,64]{2,1,0:T(8,128)} async-done(((f32[2,64,64]{2,1,0:T(8,128)}), f32[64,64,64]{2,1,0:T(8,128)}) %all-gather.7.cloned.1.call-update) | async-done | bytes 1048592 | tf_op jit(solution)/shard_map/all_gather | solution.py:16
  377.6 30.0 %while.74 = (s32[]{:T(128)}, f32[2,64,64]{2,1,0:T(8,128)S(1)}, s32[]{:T(128)}, f32[32,2]{1,0:T(8,128)S(1)}, f32[32,2,64,64]{3,2,1,0:T(8,128)}, /*index=5*/s32[]{:T(128)}, s32[]{:T(128)}) while((s32[]{:T(128)}, f32[2,64,64]{2,1,0:T(8,128)S(1)}, s32[]{:T(128)}, f32[32,2]{1,0:T(8,128)S(1)}, f32[32,2,64,64]{3,2,1,0:T(8,128)}, ...), condition=%wide.region_12.13_spmd.clone, body=%wide.region_11.12_spmd.clone.sunk | while | flops 32772 | bytes 98433 | solution.py:29
  409.3 11.8 %all-to-all-start.6 = ((bf16[16,128,128]{1,2,0:T(8,128)(2,1)}), bf16[16,128,128]{1,2,0:T(8,128)(2,1)S(1)}, u32[]{:S(2)}, u32[]{:S(2)}) async-start(bf16[16,128,128]{1,2,0:T(8,128)(2,1)} %bitcast.30), calls=%async_computation.6 | async-start | bytes 1048576 | tf_op jit(solution)/shard_map/all_to_all | solution.py:154
  424.1 14.3 %all-to-all-done.6 = bf16[16,128,128]{1,2,0:T(8,128)(2,1)S(1)} async-done(((bf16[16,128,128]{1,2,0:T(8,128)(2,1)}), bf16[16,128,128]{1,2,0:T(8,128)(2,1)S(1)}, u32[]{:S(2)}, u32[]{:S(2)}) %all-to-all-start.6) | async-done | bytes 524320 | tf_op jit(solution)/shard_map/all_to_all | solution.py:154
  (413 shorter events, 182.0 us)
Async XLA Ops:
  7.2 20.0 %all-to-all-start.4 = ((bf16[128,16,2]{0,2,1:T(2,128)(2,1)}), bf16[128,16,2]{0,2,1:T(2,128)(2,1)S(1)}, u32[]{:S(2)}, u32[]{:S(2)}) async-start(bf16[128,16,2]{0,2,1:T(2,128)(2,1)} %bitcast.263), calls=%async_computation.4 | async-start | bytes 16384 | tf_op jit(solution)/shard_map/all_to_all | solution.py:74
  20.8 16.1 %copy-start.6 = (bf16[128,2048]{1,0:T(8,128)(2,1)S(1)}, bf16[128,2048]{1,0:T(8,128)(2,1)}, u32[]{:S(2)}) copy-start(bf16[128,2048]{1,0:T(8,128)(2,1)} %param.26) | copy-start | bytes 1572868
  22.9 15.0 %copy-start.7 = (bf16[128,2048]{1,0:T(8,128)(2,1)S(1)}, bf16[128,2048]{1,0:T(8,128)(2,1)}, u32[]{:S(2)}) copy-start(bf16[128,2048]{1,0:T(8,128)(2,1)} %param.27) | copy-start | bytes 1572868
  25.0 13.9 %copy-start.8 = (bf16[128,2048]{1,0:T(8,128)(2,1)S(1)}, bf16[128,2048]{1,0:T(8,128)(2,1)}, u32[]{:S(2)}) copy-start(bf16[128,2048]{1,0:T(8,128)(2,1)} %param.28) | copy-start | bytes 1572868
  27.2 24.6 %all-to-all-start = ((bf16[128,16,128]{0,2,1:T(8,128)(2,1)}), bf16[128,16,128]{0,2,1:T(8,128)(2,1)S(1)}, u32[]{:S(2)}, u32[]{:S(2)}) async-start(bf16[128,16,128]{0,2,1:T(8,128)(2,1)} %bitcast.1), calls=%async_computation | async-start | bytes 1048576 | tf_op jit(solution)/shard_map/all_to_all | solution.py:71
  34.4 9.0 %copy-start.23 = (s32[16,16]{1,0:T(8,128)S(1)}, s32[16,16]{1,0:T(8,128)}, u32[]{:S(2)}) copy-start(s32[16,16]{1,0:T(8,128)} %param.33) | copy-start | bytes 3076
  51.7 20.2 %all-to-all-start.1 = ((bf16[128,16,128]{0,2,1:T(8,128)(2,1)}), bf16[128,16,128]{0,2,1:T(8,128)(2,1)S(1)}, u32[]{:S(2)}, u32[]{:S(2)}) async-start(bf16[128,16,128]{0,2,1:T(8,128)(2,1)} %bitcast.3), calls=%async_computation.1 | async-start | bytes 1048576 | tf_op jit(solution)/shard_map/all_to_all | solution.py:72
  71.9 20.2 %all-to-all-start.2 = ((bf16[128,16,128]{0,2,1:T(8,128)(2,1)}), bf16[128,16,128]{0,2,1:T(8,128)(2,1)S(1)}, u32[]{:S(2)}, u32[]{:S(2)}) async-start(bf16[128,16,128]{0,2,1:T(8,128)(2,1)} %bitcast.5), calls=%async_computation.2 | async-start | bytes 1048576 | tf_op jit(solution)/shard_map/all_to_all | solution.py:73
  92.1 42.9 %all-to-all-start.7 = ((bf16[128,16,128]{0,2,1:T(8,128)(2,1)}), bf16[128,16,128]{0,2,1:T(8,128)(2,1)S(1)}, u32[]{:S(2)}, u32[]{:S(2)}) async-start(bf16[128,16,128]{0,2,1:T(8,128)(2,1)} %bitcast.33), calls=%async_computation.7 | async-start | bytes 1048576 | tf_op jit(solution)/shard_map/all_to_all | solution.py:68
  99.2 5.6 %copy-start.13 = (pred[512,512]{0,1:T(8,128)(4,1)S(1)}, pred[512,512]{0,1:T(8,128)(4,1)}, u32[]{:S(2)}) copy-start(pred[512,512]{0,1:T(8,128)(4,1)} %fusion.68) | copy-start | bytes 786436
  102.1 5.3 %copy-start.16 = (bf16[512,2,64]{0,2,1:T(8,128)(2,1)S(1)}, bf16[512,2,64]{0,2,1:T(8,128)(2,1)}, u32[]{:S(2)}) copy-start(bf16[512,2,64]{0,2,1:T(8,128)(2,1)} %slice.181) | copy-start | bytes 393220
  110.9 4.5 %copy-start.18 = (bf16[512,2,64]{0,2,1:T(8,128)(2,1)S(1)}, bf16[512,2,64]{0,2,1:T(8,128)(2,1)}, u32[]{:S(2)}) copy-start(bf16[512,2,64]{0,2,1:T(8,128)(2,1)} %slice.194) | copy-start | bytes 393220
  115.4 3.8 copy-start.5
  115.4 3.8 copy-start.17
  119.2 4.3 copy-start.12
  119.2 5.4 %copy-start.10 = (bf16[4,128,128]{1,2,0:T(8,128)(2,1)S(1)}, bf16[4,128,128]{1,2,0:T(8,128)(2,1)}, u32[]{:S(2)}) copy-start(bf16[4,128,128]{1,2,0:T(8,128)(2,1)} %get-tuple-element.661) | copy-start | bytes 393220
  135.0 23.8 %all-to-all-start.5 = ((bf16[128,16,128]{0,2,1:T(8,128)(2,1)}), bf16[128,16,128]{0,2,1:T(8,128)(2,1)S(1)}, u32[]{:S(2)}, u32[]{:S(2)}) async-start(bf16[128,16,128]{0,2,1:T(8,128)(2,1)} %bitcast.19), calls=%async_computation.5 | async-start | bytes 1048576 | tf_op jit(solution)/shard_map/all_to_all | solution.py:69
  141.5 4.6 %copy-start.15 = (f32[16,128,2]{1,2,0:T(2,128)S(1)}, f32[16,128,2]{1,2,0:T(2,128)}, u32[]{:S(2)}) copy-start(f32[16,128,2]{1,2,0:T(2,128)} %copy.84) | copy-start | bytes 49156
  146.2 16.4 %copy-start.22 = (f32[2]{0:T(128)S(1)}, f32[2]{0:T(128)}, u32[]{:S(2)}) copy-start(f32[2]{0:T(128)} %custom-call.3) | copy-start | bytes 28
  158.9 31.1 %all-to-all-start.3 = ((bf16[128,16,128]{0,2,1:T(8,128)(2,1)}), bf16[128,16,128]{0,2,1:T(8,128)(2,1)S(1)}, u32[]{:S(2)}, u32[]{:S(2)}) async-start(bf16[128,16,128]{0,2,1:T(8,128)(2,1)} %bitcast.14), calls=%async_computation.3 | async-start | bytes 1048576 | tf_op jit(solution)/shard_map/all_to_all | solution.py:70
  162.3 30.6 %copy-start.21 = (f32[2]{0:T(128)S(1)}, f32[2]{0:T(128)}, u32[]{:S(2)}) copy-start(f32[2]{0:T(128)} %custom-call) | copy-start | bytes 28
  162.4 129.5 %all-gather.9.cloned.1.call-start = ((), (), s32[]{:S(2)}) async-start(), calls=%async_computation.11 | async-start | bytes 2162688 | tf_op jit(solution)/shard_map/all_gather | solution.py:16
  189.9 187.7 %all-gather.7.cloned.1.call-start = ((), (), s32[]{:S(2)}) async-start(), calls=%async_computation.10 | async-start | bytes 2162688 | tf_op jit(solution)/shard_map/all_gather | solution.py:16
  193.0 131.5 %copy-start.19 = (pred[128,128]{1,0:T(8,128)(4,1)S(1)}, pred[128,128]{1,0:T(8,128)(4,1)}, u32[]{:S(2)}) copy-start(pred[128,128]{1,0:T(8,128)(4,1)} %iota_compare_fusion.2) | copy-start | bytes 49156
  193.0 131.5 %copy-start.20 = (f32[16,2,128]{2,1,0:T(2,128)S(1)}, f32[16,2,128]{2,1,0:T(2,128)}, u32[]{:S(2)}) copy-start(f32[16,2,128]{2,1,0:T(2,128)} %copy.81) | copy-start | bytes 49156
  229.3 62.5 %copy-start = (f32[2,64,64]{2,1,0:T(8,128)}, f32[2,64,64]{2,1,0:T(8,128)S(1)}, u32[]{:S(2)}) copy-start(f32[2,64,64]{2,1,0:T(8,128)S(1)} %get-tuple-element.471) | copy-start | bytes 98308
  327.6 37.4 %all-to-all-start.9 = ((bf16[16,128,128]{1,2,0:T(8,128)(2,1)}), bf16[16,128,128]{1,2,0:T(8,128)(2,1)}, u32[]{:S(2)}, u32[]{:S(2)}) async-start(bf16[16,128,128]{1,2,0:T(8,128)(2,1)} %bitcast.255), calls=%async_computation.9 | async-start | bytes 1048576 | tf_op jit(solution)/shard_map/all_to_all | solution.py:156
  349.6 3.9 copy-start.3
  353.5 54.1 %copy-start.2 = (f32[16,128,2,64]{1,3,2,0:T(8,128)S(1)}, f32[16,128,2,64]{1,3,2,0:T(8,128)}, u32[]{:S(2)}) copy-start(f32[16,128,2,64]{1,3,2,0:T(8,128)} %convolution_bitcast_fusion.4) | copy-start | bytes 3145732
  353.5 54.1 %copy-start.4 = (f32[16,2,64,64]{3,2,1,0:T(8,128)S(1)}, f32[16,2,64,64]{3,2,1,0:T(8,128)}, u32[]{:S(2)}) copy-start(f32[16,2,64,64]{3,2,1,0:T(8,128)} %get-tuple-element.473) | copy-start | bytes 1572868
  365.0 44.2 %all-to-all-start.8 = ((bf16[16,128,128]{1,2,0:T(8,128)(2,1)}), bf16[16,128,128]{1,2,0:T(8,128)(2,1)S(1)}, u32[]{:S(2)}, u32[]{:S(2)}) async-start(bf16[16,128,128]{1,2,0:T(8,128)(2,1)} %bitcast.254), calls=%async_computation.8 | async-start | bytes 1048576 | tf_op jit(solution)/shard_map/all_to_all | solution.py:155
  409.3 29.1 %all-to-all-start.6 = ((bf16[16,128,128]{1,2,0:T(8,128)(2,1)}), bf16[16,128,128]{1,2,0:T(8,128)(2,1)S(1)}, u32[]{:S(2)}, u32[]{:S(2)}) async-start(bf16[16,128,128]{1,2,0:T(8,128)(2,1)} %bitcast.30), calls=%async_computation.6 | async-start | bytes 1048576 | tf_op jit(solution)/shard_map/all_to_all | solution.py:154
  (4 other events, 9.4 us)
Sparse Core Ops, SparseCore 0:
  190.0 79.8 all-gather.8
  292.0 85.5 all-gather.6
where the time goes:
time: 453 us; the launch traced here: 446 us
  other arithmetic  127 us (28%)
  starting transfers between devices  75 us (17%)
  waiting for transfers between devices  71.6 us (16%)
  blocking collectives  61.9 us (14%)
  matrix products  49.5 us (11%)
  local copies, waits for them, and re-layouts  44 us (10%)
  between operations  15.2 us (3%)
    unnamed x1, blocking collectives  61.9 us
    select_n x64, other arithmetic, lap(): return jax.tree.map(lambda a, b: jnp.where(reached, a, b), new, before)  59 us
    add x32, other arithmetic, combine_pairs(): later[0][:, None, None] * earlier[1] + later[1]  29.4 us
    dot_general x8, matrix products, mixing(): return jnp.einsum(form, left, right, preferred_element_type=jnp.float32)  25.2 us
    mul x32, other arithmetic, combine_pairs(): earlier[0] * later[0]  22.3 us
    all_to_all x1, starting transfers between devices, body(): lax.all_to_all(grad_v_one, 'head', split_axis=0, concat_axis=1, tiled=True)  20 us
    sub x4, matrix products, body(): powers = jnp.exp(scores - highest)  15.9 us
    all_to_all x1, waiting for transfers between devices, body(): lax.all_to_all(grad_q_one, 'head', split_axis=0, concat_axis=1, tiled=True)  14.3 us
  transfers between devices with their start and end apart: 12, of which 7 were waited for; matrix products, arithmetic and copies ran while one was open for 49% of the time, Pallas kernels for 0%

commit v1 on v0

v1 whole, which is shorter than its diff:
```python
import functools
import math

import jax
import jax.numpy as jnp
from jax import lax
from jax.experimental import pallas as pl
from jax.experimental.pallas import tpu as pltpu
from jax.sharding import PartitionSpec as P

T = 128
W = 128
HD = 64
MSG = 80
LOW = -1e30
F32 = jnp.float32
BF16 = jnp.bfloat16
MESH = pl.DeviceIdType.MESH


def dot(a, b, ca=1, cb=0):
    return lax.dot_general(a, b, (((ca,), (cb,)), ((), ())), preferred_element_type=F32)


def dot_split(a, b, ca=1, cb=0):
    high = a.astype(BF16)
    low = (a - high.astype(F32)).astype(BF16)
    return dot(high, b, ca, cb) + dot(low, b, ca, cb)


def halves(x):
    first = lax.broadcasted_iota(jnp.int32, x.shape, 1) < HD
    zero = jnp.zeros_like(x)
    return jnp.concatenate([jnp.where(first, x, zero), jnp.where(first, zero, x)], axis=0)


def fold(x):
    first = lax.broadcasted_iota(jnp.int32, (HD, W), 1) < HD
    return jnp.where(first, x[:HD], x[HD:])


def total_rows(total):
    high = total.astype(BF16).astype(F32)
    rest = total - high
    mid = rest.astype(BF16).astype(F32)
    low = rest - mid
    row = lax.broadcasted_iota(jnp.int32, (MSG - HD, W), 0)
    rows = jnp.where(row == 0, high, jnp.where(row == 1, mid, jnp.where(row == 2, low, 0.0)))
    return rows.astype(BF16)


def read_total(rows):
    return jnp.sum(rows.astype(F32), axis=0, keepdims=True)


def kernel(
    n_ctx,
    n,
    lq_ref,
    lk_ref,
    lv_ref,
    sq_ref,
    sk_ref,
    up_ref,
    dec_ref,
    mask_ref,
    gq_ref,
    gk_ref,
    gv_ref,
    k_buf,
    q_buf,
    u_buf,
    lg_buf,
    lg_out,
    bs_buf,
    bs_out,
    st_buf,
    st_out,
    re_buf,
    re_out,
    ri_buf,
    ri_out,
    c1_buf,
    c1_out,
    c2_buf,
    c2_out,
    weights,
    mixed,
    entries,
    leaving,
    scores,
    probs,
    loc_a,
    loc_b,
    acc_q,
    acc_k,
    acc_v,
    send_in,
    recv_in,
    send_mat,
    recv_mat,
    send_ctx,
    recv_ctx,
):
    here = lax.axis_index("ctx")
    me = lax.axis_index("head")
    chunks = n // 2
    scale = 1.0 / (HD * math.sqrt(HD))
    root_log2 = math.log2(math.e) / math.sqrt(HD)

    def peer_at(i):
        half = (i + 1) // 2
        odd = i % 2
        off = odd * half + (1 - odd) * (n - half)
        return (me + off) % n

    def lanes(p):
        return pl.ds(pl.multiple_of(p * W, W), W)

    def rounds(low, high, step, *carry):
        if carry:
            return lax.fori_loop(low, high, step, *carry)

        def plain(i, nothing):
            step(i)
            return nothing

        lax.fori_loop(low, high, plain, 0)

    barrier = pltpu.get_barrier_semaphore()

    def greet_head(i):
        pl.semaphore_signal(
            barrier, inc=1, device_id=(here, (me + i) % n), device_id_type=MESH
        )

    def greet_ctx(i):
        pl.semaphore_signal(
            barrier, inc=1, device_id=((here + i) % n_ctx, me), device_id_type=MESH
        )

    rounds(1, n, greet_head)
    rounds(1, n_ctx, greet_ctx)
    pl.semaphore_wait(barrier, n - 1 + n_ctx - 1)

    def in_copy(which, src, buf, peer, slot):
        return pltpu.make_async_remote_copy(
            src_ref=src.at[:, lanes(peer)],
            dst_ref=buf.at[slot],
            send_sem=send_in.at[which, peer],
            recv_sem=recv_in.at[which, slot],
            device_id=(here, peer),
            device_id_type=MESH,
        )

    def mat_copy(which, src, buf, peer, slot):
        return pltpu.make_async_remote_copy(
            src_ref=src.at[peer],
            dst_ref=buf.at[slot],
            send_sem=send_mat.at[which, peer],
            recv_sem=recv_mat.at[which, slot],
            device_id=(here, peer),
            device_id_type=MESH,
        )

    def ctx_copy(which, src, buf, peer, slot):
        return pltpu.make_async_remote_copy(
            src_ref=src,
            dst_ref=buf.at[slot],
            send_sem=send_ctx.at[which, peer],
            recv_sem=recv_ctx.at[which, slot],
            device_id=(peer, me),
            device_id_type=MESH,
        )

    inputs = ((sk_ref, k_buf), (sq_ref, q_buf), (up_ref, u_buf))
    for which, (src, buf) in enumerate(inputs):
        rounds(1, n, lambda i: in_copy(which, src, buf, peer_at(i), me).start())
        buf[me] = src[:, lanes(me)]

    tri = jnp.where(
        lax.broadcasted_iota(jnp.int32, (T, T), 1) <= lax.broadcasted_iota(jnp.int32, (T, T), 0),
        1.0,
        0.0,
    ).astype(BF16)

    def prepare(i):
        p = peer_at(i)
        heads = dec_ref.shape[1]
        columns, rows = [], []
        for h in range(2):
            pick = jnp.where(
                lax.broadcasted_iota(jnp.int32, (heads, T), 0) == 2 * p + h, 1.0, 0.0
            ).astype(BF16)
            spread_out = dot(dec_ref[...], pick).astype(BF16)
            columns.append(dot(tri, spread_out))
            rows.append(dot(spread_out, tri, 0, 1))
        lower = lax.broadcasted_iota(jnp.int32, (T, T), 1) <= lax.broadcasted_iota(
            jnp.int32, (T, T), 0
        )
        table = jnp.concatenate(
            [
                jnp.where(lower, jnp.exp(jnp.minimum(rows[h] - columns[h], 0.0)), 0.0)
                for h in range(2)
            ],
            axis=0,
        )
        weights[p] = table
        first = lax.broadcasted_iota(jnp.int32, (T, W), 1) < HD
        level = jnp.where(first, columns[0], columns[1])
        last = level[T - 1 : T]
        entries[p] = jnp.exp(-level)
        leave = jnp.exp(level - last)
        leaving[p] = leave
        lk = lk_ref[:, lanes(p)]
        lv = lv_ref[:, lanes(p)]
        sums = fold(dot_split(lk.astype(F32) * leave, lv, 0, 0))
        bs_out[p, :HD] = sums.astype(BF16)
        bs_out[p, HD:] = total_rows(jnp.exp(-last))

        @pl.when(i > 0)
        def _():
            mat_copy(0, bs_out, bs_buf, p, me).start()

        pair = dot(halves(lq_ref[:, lanes(p)]), lk, 1, 1)
        mixed[p] = (pair * table).astype(BF16)

    rounds(0, n, prepare)
    bs_buf[me] = bs_out[me]

    for which in range(2):
        src, buf = inputs[which]
        rounds(1, n, lambda i: in_copy(which, src, buf, peer_at(i), peer_at(i)).wait_recv())

    def soften(t):
        both = halves(q_buf[t])
        size = 2 * T

        def block_bias(c):
            upper = (mask_ref[t, 2 * c].astype(F32) - 1.0) * (-LOW)
            lower = (mask_ref[t, 2 * c + 1].astype(F32) - 1.0) * (-LOW)
            row = lax.broadcasted_iota(jnp.int32, (size, size), 0)
            return jnp.where(row < T, upper, lower)

        def score(c):
            keys = jnp.concatenate([k_buf[2 * c], k_buf[2 * c + 1]], axis=0)
            return dot(keys, both, 1, 1) + block_bias(c)

        def peak(x):
            return jnp.max(x.reshape(size // 8, 8, size), axis=0)

        def first_pass(c, highest):
            x = score(c)
            scores[c] = x
            return jnp.maximum(highest, peak(x))

        last = t // 2
        highest = rounds(0, last, first_pass, jnp.full((8, size), LOW, F32))
        key = last * size + lax.broadcasted_iota(jnp.int32, (size, size), 0)
        query = t * T + lax.broadcasted_iota(jnp.int32, (size, size), 1) % T
        x = jnp.where(key <= query, score(last), LOW)
        scores[last] = x
        highest = jnp.maximum(highest, peak(x))
        highest = jnp.max(highest, axis=0, keepdims=True)

        def second_pass(c, total):
            e = jnp.exp2((scores[c] - highest) * root_log2)
            scores[c] = e
            return total + jnp.sum(e.reshape(size // 8, 8, size), axis=0)

        total = rounds(0, last + 1, second_pass, jnp.zeros((8, size), F32))
        inverse = 1.0 / jnp.sum(total, axis=0, keepdims=True)

        def third_pass(c):
            probs[c, t] = (scores[c] * inverse).astype(BF16)

        rounds(0, last + 1, third_pass)

    rounds(0, n, soften)

    rounds(1, n, lambda i: in_copy(2, up_ref, u_buf, peer_at(i), peer_at(i)).wait_recv())

    my_chunk = me // 2

    def light(i):
        half = (i + 1) // 2
        odd = i % 2
        off = odd * half + (1 - odd) * (chunks - half)
        c = (my_chunk + off) % chunks

        def add(t, acc):
            return acc + dot(probs[c, t], halves(u_buf[t]))

        grad = rounds(2 * c, n, add, jnp.zeros((2 * T, W), F32)).astype(BF16)
        lg_out[2 * c] = grad[:T]
        lg_out[2 * c + 1] = grad[T:]
        for side in range(2):

            @pl.when(2 * c + side != me)
            def _():
                mat_copy(1, lg_out, lg_buf, 2 * c + side, me).start()

    rounds(0, chunks, light)
    lg_buf[me] = lg_out[me]

    zero_b = jnp.zeros((HD, W), F32)
    one_a = jnp.ones((1, W), F32)
    rounds(1, n, lambda i: mat_copy(0, bs_out, bs_buf, peer_at(i), peer_at(i)).wait_recv())

    def forward(b, carried):
        a, s = carried
        loc_a[0, b] = jnp.broadcast_to(a, (8, W))
        loc_b[0, b] = s
        total = read_total(bs_buf[b, HD:])
        return a * total, total * s + bs_buf[b, :HD].astype(F32)

    a, s = rounds(0, n, forward, (one_a, zero_b))
    c1_out[:HD] = s.astype(BF16)
    c1_out[HD:] = total_rows(a)
    rounds(here + 1, n_ctx, lambda k: ctx_copy(0, c1_out, c1_buf, k, here).start())

    def reach(i):
        p = peer_at(i)

        @pl.when(i > 0)
        def _():
            mat_copy(1, lg_out, lg_buf, p, p).wait_recv()

        moved = lq_ref[:, lanes(p)].astype(F32) * entries[p]
        re_out[p] = fold(dot_split(moved, lg_buf[p], 0, 0)).astype(BF16)

        @pl.when(i > 0)
        def _():
            mat_copy(2, re_out, re_buf, p, me).start()

    rounds(0, n, reach)
    re_buf[me] = re_out[me]

    def gather_forward(k, s):
        ctx_copy(0, c1_out, c1_buf, k, k).wait_recv()
        return read_total(c1_buf[k, HD:]) * s + c1_buf[k, :HD].astype(F32)

    span_in = rounds(0, here, gather_forward, zero_b)

    def send_state(i):
        b = peer_at(i)
        st_out[b] = (loc_a[0, b, :1] * span_in + loc_b[0, b]).astype(BF16)

        @pl.when(i > 0)
        def _():
            mat_copy(3, st_out, st_buf, b, me).start()

    rounds(0, n, send_state)
    st_buf[me] = st_out[me]

    rounds(1, n, lambda i: mat_copy(2, re_out, re_buf, peer_at(i), peer_at(i)).wait_recv())

    def backward(j, carried):
        b = n - 1 - j
        a, s = carried
        loc_a[1, b] = jnp.broadcast_to(a, (8, W))
        loc_b[1, b] = s
        total = read_total(bs_buf[b, HD:])
        return a * total, total * s + re_buf[b].astype(F32)

    a, s = rounds(0, n, backward, (one_a, zero_b))
    c2_out[:HD] = s.astype(BF16)
    c2_out[HD:] = total_rows(a)
    rounds(0, here, lambda k: ctx_copy(1, c2_out, c2_buf, k, here).start())

    def inside(p):
        lg2 = halves(lg_buf[p])
        lk = lk_ref[:, lanes(p)]
        lq = lq_ref[:, lanes(p)]
        back = (dot(lg2, lv_ref[:, lanes(p)], 1, 1) * weights[p]).astype(BF16)
        wide = jnp.concatenate([back[:T], back[T:]], axis=1)
        acc_q[p] = dot(wide, halves(lk))
        acc_k[p] = dot(back, halves(lq), 0, 0)
        acc_v[p] = dot(mixed[p], lg2, 0, 0)

    rounds(0, n, inside)

    def gather_backward(j, s):
        k = n_ctx - 1 - j
        ctx_copy(1, c2_out, c2_buf, k, k).wait_recv()
        return read_total(c2_buf[k, HD:]) * s + c2_buf[k, :HD].astype(F32)

    span_back = rounds(0, n_ctx - 1 - here, gather_backward, zero_b)

    def send_reach(i):
        b = peer_at(i)
        ri_out[b] = (loc_a[1, b, :1] * span_back + loc_b[1, b]).astype(BF16)

        @pl.when(i > 0)
        def _():
            mat_copy(4, ri_out, ri_buf, b, me).start()

    rounds(0, n, send_reach)
    ri_buf[me] = ri_out[me]

    def finish_query(i):
        p = peer_at(i)

        @pl.when(i > 0)
        def _():
            mat_copy(3, st_out, st_buf, p, p).wait_recv()

        carried = dot(lg_buf[p], halves(st_buf[p]), 1, 1)
        gq_ref[:, lanes(p)] = (scale * (acc_q[p] + entries[p] * carried)).astype(BF16)

    rounds(0, n, finish_query)

    def finish(i):
        p = peer_at(i)

        @pl.when(i > 0)
        def _():
            mat_copy(4, ri_out, ri_buf, p, p).wait_recv()

        both = halves(ri_buf[p])
        leave = leaving[p]
        from_value = dot(lv_ref[:, lanes(p)], both, 1, 1)
        from_key = dot(lk_ref[:, lanes(p)], both)
        gk_ref[:, lanes(p)] = (scale * (acc_k[p] + leave * from_value)).astype(BF16)
        gv_ref[:, lanes(p)] = (scale * (acc_v[p] + leave * from_key)).astype(BF16)

    rounds(0, n, finish)

    def drain(i):
        p = peer_at(i)
        for which, (src, buf) in enumerate(inputs):
            in_copy(which, src, buf, p, me).wait_send()
        mats = ((bs_out, bs_buf), (lg_out, lg_buf), (re_out, re_buf), (st_out, st_buf), (ri_out, ri_buf))
        for which, (src, buf) in enumerate(mats):
            mat_copy(which, src, buf, p, me).wait_send()

    rounds(1, n, drain)
    rounds(here + 1, n_ctx, lambda k: ctx_copy(0, c1_out, c1_buf, k, here).wait_send())
    rounds(0, here, lambda k: ctx_copy(1, c2_out, c2_buf, k, here).wait_send())


def body(n_ctx, n, *args):
    shape = args[0].shape
    vmem = pl.BlockSpec(memory_space=pltpu.VMEM)
    chunks = n // 2
    pairs = (n, T, W)
    mats = (n, HD, W)
    scratch = [
        pltpu.VMEM(pairs, BF16),
        pltpu.VMEM(pairs, BF16),
        pltpu.VMEM(pairs, BF16),
        pltpu.VMEM(pairs, BF16),
        pltpu.VMEM(pairs, BF16),
        pltpu.VMEM((n, MSG, W), BF16),
        pltpu.VMEM((n, MSG, W), BF16),
        pltpu.VMEM(mats, BF16),
        pltpu.VMEM(mats, BF16),
        pltpu.VMEM(mats, BF16),
        pltpu.VMEM(mats, BF16),
        pltpu.VMEM(mats, BF16),
        pltpu.VMEM(mats, BF16),
        pltpu.VMEM((n_ctx, MSG, W), BF16),
        pltpu.VMEM((MSG, W), BF16),
        pltpu.VMEM((n_ctx, MSG, W), BF16),
        pltpu.VMEM((MSG, W), BF16),
        pltpu.VMEM((n, 2 * T, T), F32),
        pltpu.VMEM((n, 2 * T, T), BF16),
        pltpu.VMEM(pairs, F32),
        pltpu.VMEM(pairs, F32),
        pltpu.VMEM((chunks, 2 * T, 2 * T), F32),
        pltpu.VMEM((chunks, n, 2 * T, 2 * T), BF16),
        pltpu.VMEM((2, n, 8, W), F32),
        pltpu.VMEM((2, n, HD, W), F32),
        pltpu.VMEM(pairs, F32),
        pltpu.VMEM(pairs, F32),
        pltpu.VMEM(pairs, F32),
        pltpu.SemaphoreType.DMA((3, n)),
        pltpu.SemaphoreType.DMA((3, n)),
        pltpu.SemaphoreType.DMA((5, n)),
        pltpu.SemaphoreType.DMA((5, n)),
        pltpu.SemaphoreType.DMA((2, n_ctx)),
        pltpu.SemaphoreType.DMA((2, n_ctx)),
    ]
    return pl.pallas_call(
        functools.partial(kernel, n_ctx, n),
        out_shape=[jax.ShapeDtypeStruct(shape, BF16)] * 3,
        in_specs=[vmem] * 7 + [pl.BlockSpec(memory_space=pltpu.SMEM)],
        out_specs=[vmem] * 3,
        scratch_shapes=scratch,
        compiler_params=pltpu.CompilerParams(
            collective_id=0, has_side_effects=True, vmem_limit_bytes=56 * 1024 * 1024
        ),
        name="span_backward",
    )(*args)


def solution(mesh):
    tokens = P(("ctx", "head"), None)
    return jax.shard_map(
        functools.partial(body, mesh.shape["ctx"], mesh.shape["head"]),
        mesh=mesh,
        in_specs=(tokens,) * 7 + (P("ctx", None),),
        out_specs=(tokens,) * 3,
        check_vma=False,
    )
```

time: 453 us -> 130 us (0.29)
  the two profiles are of different devices: /device:TPU:1 before, /device:TPU:23 now
where the time goes in v1:
time: 130 us
  Pallas kernels  124 us (95%)
  local copies, waits for them, and re-layouts  5.38 us (4%)
    pallas_call x1, Pallas kernels, body(): pl.pallas_call(functools.partial(kernel, n_ctx, n), out_shape=[jax.ShapeD...  124 us
    unnamed x8, local copies, waits for them, and re-layouts  5.38 us

profile of v1, /device:TPU:23, one launch (start us, length us, event | category | flops | bytes accessed | tf_op | source)
XLA Modules:
  0.0 130.0 jit_solution(4980284823313914570)
XLA Ops:
  0.6 1.4 %copy.11.dec_ref = bf16[128,32]{1,0:T(8,128)(2,1)} copy(bf16[128,32]{0,1:T(8,128)(2,1)} %param.14) | data formatting | bytes 16384 | tf_op args[6]
  2.0 124.0 %span_backward.1 = (bf16[128,2048]{1,0:T(8,128)(2,1)}, bf16[128,2048]{1,0:T(8,128)(2,1)}, bf16[128,2048]{1,0:T(8,128)(2,1)}) custom-call(bf16[128,2048]{1,0:T(8,128)(2,1)} %lq_ref.1, bf16[128,2048]{1,0:T(8,128)(2,1)} %lk_ref.1, bf16[128,2048]{1,0:T(8,128)(2,1)} %lv_ref.1, bf16[128,2048]{1,0:T(8,128)(2,1)} %sq_ref.1, bf16[128,2048]{1,0:T(8,128)(2,1)} %sk_ref.1, ...), custom_call_target="tpu_custom_call" | custom-call | tf_op jit(solution)/shard_map/span_backward/pallas_call | solution.py:484
  126.0 0.0 copy-start.1
  126.0 1.9 %copy.15 = bf16[128,2048]{1,0:T(8,128)(2,1)} copy(bf16[128,2048]{1,0:T(8,128)(2,1)} %get-tuple-element.6) | data formatting | bytes 1048576
  128.0 0.0 copy-done.1
  128.0 0.0 copy-start
  128.0 0.8 copy.16
  128.8 0.4 copy-done
  129.2 0.8 copy.17
Async XLA Ops:
  126.0 2.0 %copy-start.1 = (bf16[128,2048]{1,0:T(8,128)(2,1)S(1)}, bf16[128,2048]{1,0:T(8,128)(2,1)}, u32[]{:S(2)}) copy-start(bf16[128,2048]{1,0:T(8,128)(2,1)} %get-tuple-element.7) | copy-start | bytes 1572868
  128.0 1.2 copy-start

commit v2 on v1

v2 whole, which is shorter than its diff:
```python
import functools
import math

import jax
import jax.numpy as jnp
from jax import lax
from jax.experimental import pallas as pl
from jax.experimental.pallas import tpu as pltpu
from jax.sharding import PartitionSpec as P

T = 128
W = 128
HD = 64
MSG = 80
LOW = -1e30
F32 = jnp.float32
BF16 = jnp.bfloat16
MESH = pl.DeviceIdType.MESH


def dot(a, b, ca=1, cb=0):
    return lax.dot_general(a, b, (((ca,), (cb,)), ((), ())), preferred_element_type=F32)


def dot_split(a, b, ca=1, cb=0):
    high = a.astype(BF16)
    low = (a - high.astype(F32)).astype(BF16)
    return dot(high, b, ca, cb) + dot(low, b, ca, cb)


def halves(x):
    first = lax.broadcasted_iota(jnp.int32, x.shape, 1) < HD
    zero = jnp.zeros_like(x)
    return jnp.concatenate([jnp.where(first, x, zero), jnp.where(first, zero, x)], axis=0)


def fold(x):
    first = lax.broadcasted_iota(jnp.int32, (HD, W), 1) < HD
    return jnp.where(first, x[:HD], x[HD:])


def total_rows(total):
    high = total.astype(BF16).astype(F32)
    rest = total - high
    mid = rest.astype(BF16).astype(F32)
    low = rest - mid
    row = lax.broadcasted_iota(jnp.int32, (MSG - HD, W), 0)
    rows = jnp.where(row == 0, high, jnp.where(row == 1, mid, jnp.where(row == 2, low, 0.0)))
    return rows.astype(BF16)


def read_total(rows):
    return jnp.sum(rows.astype(F32), axis=0, keepdims=True)


def kernel(
    n_ctx,
    n_y,
    n,
    lq_ref,
    lk_ref,
    lv_ref,
    sq_ref,
    sk_ref,
    up_ref,
    dec_ref,
    mask_ref,
    gq_ref,
    gk_ref,
    gv_ref,
    k_buf,
    q_buf,
    u_buf,
    lg_buf,
    lg_out,
    bs_buf,
    bs_out,
    st_buf,
    st_out,
    mv_buf,
    mv_out,
    ri_buf,
    ri_out,
    row_buf,
    row_out,
    col_buf,
    col_out,
    weights,
    level_rows,
    level_columns,
    reaches,
    u_wide,
    mixed,
    entries,
    leaving,
    scores,
    probs,
    loc_a,
    loc_b,
    acc_q,
    acc_k,
    acc_v,
    send_in,
    recv_in,
    send_mat,
    recv_mat,
    send_row,
    recv_row,
    send_col,
    recv_col,
):
    here = lax.axis_index("ctx")
    me = lax.axis_index("head")
    n_x = n_ctx // n_y
    x, y = here // n_y, here % n_y
    chunks = n // 2
    scale = 1.0 / (HD * math.sqrt(HD))
    root_log2 = math.log2(math.e) / math.sqrt(HD)

    def peer_at(i):
        half = (i + 1) // 2
        odd = i % 2
        off = odd * half + (1 - odd) * (n - half)
        return (me + off) % n

    def lanes(p):
        return pl.ds(pl.multiple_of(p * W, W), W)

    def rounds(low, high, step, *carry):
        if carry:
            return lax.fori_loop(low, high, step, *carry)

        def plain(i, nothing):
            step(i)
            return nothing

        lax.fori_loop(low, high, plain, 0)

    barrier = pltpu.get_barrier_semaphore()

    def greet_head(i):
        pl.semaphore_signal(
            barrier, inc=1, device_id=(here, (me + i) % n), device_id_type=MESH
        )

    def greet_ctx(k):
        pl.semaphore_signal(barrier, inc=1, device_id=(k, me), device_id_type=MESH)

    rounds(1, n, greet_head)
    rounds(1, n_y, lambda i: greet_ctx(x * n_y + (y + i) % n_y))
    rounds(1, n_x, lambda i: greet_ctx((x + i) % n_x * n_y + y))
    pl.semaphore_wait(barrier, n - 1 + n_y - 1 + n_x - 1)

    def in_copy(which, src, buf, peer, slot):
        return pltpu.make_async_remote_copy(
            src_ref=src.at[:, lanes(peer)],
            dst_ref=buf.at[slot],
            send_sem=send_in.at[which, peer],
            recv_sem=recv_in.at[which, slot],
            device_id=(here, peer),
            device_id_type=MESH,
        )

    def mat_copy(which, src, buf, peer, slot):
        return pltpu.make_async_remote_copy(
            src_ref=src.at[peer],
            dst_ref=buf.at[slot],
            send_sem=send_mat.at[which, peer],
            recv_sem=recv_mat.at[which, slot],
            device_id=(here, peer),
            device_id_type=MESH,
        )

    def row_copy(which, peer, slot):
        return pltpu.make_async_remote_copy(
            src_ref=row_out.at[which],
            dst_ref=row_buf.at[which, slot],
            send_sem=send_row.at[which, peer],
            recv_sem=recv_row.at[which, slot],
            device_id=(x * n_y + peer, me),
            device_id_type=MESH,
        )

    def col_copy(which, peer, slot):
        return pltpu.make_async_remote_copy(
            src_ref=col_out.at[which],
            dst_ref=col_buf.at[which, slot],
            send_sem=send_col.at[which, peer],
            recv_sem=recv_col.at[which, slot],
            device_id=(peer * n_y + y, me),
            device_id_type=MESH,
        )

    def pack(ref, a, s):
        ref[:HD] = s.astype(BF16)
        ref[HD:] = total_rows(a)

    def absorb(ref, carried):
        a, s = carried
        total = read_total(ref[HD:])
        return a * total, total * s + ref[:HD].astype(F32)

    def start_rows(which, a, s):
        pack(row_out.at[which], a, s)
        row_buf[which, y] = row_out[which]
        rounds(1, n_y, lambda i: row_copy(which, (y + i) % n_y, y).start())

    def fold_rows(which):
        def arrive(i):
            k = (y + i) % n_y
            row_copy(which, k, k).wait_recv()

        rounds(1, n_y, arrive)

        def step(i, carried):
            return absorb(row_buf.at[which, n_y - 1 - i if which else i], carried)

        mine = n_y - 1 - y if which else y
        part = rounds(0, mine, step, (one_a, zero_b))
        whole = rounds(mine, n_y, step, part)
        pack(col_out.at[which], *whole)
        low, high = (0, x) if which else (x + 1, n_x)
        rounds(low, high, lambda k: col_copy(which, k, x).start())
        return part

    def fold_columns(which, part):
        def step(i, carried):
            k = n_x - 1 - i if which else i
            col_copy(which, k, k).wait_recv()
            return absorb(col_buf.at[which, k], carried)

        other = rounds(0, n_x - 1 - x if which else x, step, (one_a, zero_b))
        return part[0] * other[1] + part[1]

    zero_b = jnp.zeros((HD, W), F32)
    one_a = jnp.ones((1, W), F32)
    inputs = ((sk_ref, k_buf), (sq_ref, q_buf), (up_ref, u_buf))
    for which, (src, buf) in enumerate(inputs):
        rounds(1, n, lambda i: in_copy(which, src, buf, peer_at(i), me).start())
        buf[me] = src[:, lanes(me)]

    lower = lax.broadcasted_iota(jnp.int32, (T, T), 1) <= lax.broadcasted_iota(
        jnp.int32, (T, T), 0
    )
    tri = jnp.where(lower, 1.0, 0.0).astype(BF16)
    heads = dec_ref.shape[0]
    level_rows[...] = dot(dec_ref[...], tri, 1, 1)

    def level_up(p):
        pick = jnp.where(
            lax.broadcasted_iota(jnp.int32, (heads, 2 * T), 0)
            == 2 * p + lax.broadcasted_iota(jnp.int32, (heads, 2 * T), 1) // T,
            1.0,
            0.0,
        ).astype(BF16)
        level_columns[p] = dot(tri, dot(dec_ref[...], pick, 0, 0).astype(BF16))

    for p in range(n):
        level_up(p)

    def prepare(i):
        p = peer_at(i)
        columns = [level_columns[p, :, h * T : (h + 1) * T] for h in range(2)]
        table = jnp.concatenate(
            [
                jnp.where(
                    lower,
                    jnp.exp(jnp.minimum(level_rows[pl.ds(2 * p + h, 1)] - columns[h], 0.0)),
                    0.0,
                )
                for h in range(2)
            ],
            axis=0,
        )
        weights[p] = table
        first = lax.broadcasted_iota(jnp.int32, (T, W), 1) < HD
        level = jnp.where(first, columns[0], columns[1])
        last = level[T - 1 : T]
        enter = jnp.exp(-level)
        entries[p] = enter
        leave = jnp.exp(level - last)
        leaving[p] = leave
        lk = lk_ref[:, lanes(p)]
        lv = lv_ref[:, lanes(p)]
        lq = lq_ref[:, lanes(p)]
        sums = fold(dot_split(lk.astype(F32) * leave, lv, 0, 0))
        bs_out[p, :HD] = sums.astype(BF16)
        bs_out[p, HD:] = total_rows(jnp.exp(-last))

        mv_out[p] = (lq.astype(F32) * enter).T.astype(BF16)

        @pl.when(i > 0)
        def _():
            mat_copy(2, mv_out, mv_buf, p, me).start()

        mixed[p] = (dot(halves(lq), lk, 1, 1) * table).astype(BF16)

    rounds(0, n, prepare)
    mv_buf[me] = mv_out[me]
    bs_buf[me] = bs_out[me]
    rounds(1, n, lambda i: mat_copy(0, bs_out, bs_buf, peer_at(i), me).start())

    for which in range(2):
        src, buf = inputs[which]
        rounds(1, n, lambda i: in_copy(which, src, buf, peer_at(i), peer_at(i)).wait_recv())

    def soften(u):
        size = 2 * T
        wide = 2 * size
        both = jnp.concatenate([halves(q_buf[2 * u]), halves(q_buf[2 * u + 1])], axis=0)

        def bias(c, a, b):
            return (mask_ref[2 * u + b, 2 * c + a].astype(F32) - 1.0) * (-LOW)

        def peak(x):
            return jnp.max(x.reshape(T // 8, 8, size), axis=0)

        def score(c):
            keys = k_buf[pl.ds(2 * c, 2)].reshape(size, W)
            return dot(keys, both, 1, 1)

        def part(x, a, b):
            return x[a * T : (a + 1) * T, b * size : (b + 1) * size]

        def keep(c, parts):
            for a in range(2):
                for b in range(2):
                    scores[c, a * T : (a + 1) * T, b * size : (b + 1) * size] = parts[a][b]
            return jnp.concatenate(
                [jnp.maximum(peak(parts[0][b]), peak(parts[1][b])) for b in range(2)], axis=1
            )

        def first_pass(c, highest):
            x = score(c)
            parts = [[part(x, a, b) + bias(c, a, b) for b in range(2)] for a in range(2)]
            return jnp.maximum(highest, keep(c, parts))

        highest = rounds(0, u, first_pass, jnp.full((8, wide), LOW, F32))
        key = lax.broadcasted_iota(jnp.int32, (T, size), 0)
        query = lax.broadcasted_iota(jnp.int32, (T, size), 1) % T
        x = score(u)
        parts = [
            [
                jnp.where(key <= query, part(x, 0, 0) + bias(u, 0, 0), LOW),
                part(x, 0, 1) + bias(u, 0, 1),
            ],
            [
                jnp.full((T, size), LOW, F32),
                jnp.where(key <= query, part(x, 1, 1) + bias(u, 1, 1), LOW),
            ],
        ]
        highest = jnp.maximum(highest, keep(u, parts))
        highest = jnp.max(highest, axis=0, keepdims=True)

        def second_pass(c, total):
            e = jnp.exp2((scores[c] - highest) * root_log2)
            scores[c] = e
            return total + jnp.sum(e.reshape(size // 8, 8, wide), axis=0)

        total = rounds(0, u + 1, second_pass, jnp.zeros((8, wide), F32))
        inverse = 1.0 / jnp.sum(total, axis=0, keepdims=True)

        def third_pass(c):
            probs[c, u] = (scores[c] * inverse).astype(BF16)

        rounds(0, u + 1, third_pass)

    rounds(0, chunks, soften)

    rounds(1, n, lambda i: in_copy(2, up_ref, u_buf, peer_at(i), peer_at(i)).wait_recv())

    def widen(u):
        u_wide[u] = jnp.concatenate([halves(u_buf[2 * u]), halves(u_buf[2 * u + 1])], axis=0)

    rounds(0, chunks, widen)

    my_chunk = me // 2

    def light(i):
        half = (i + 1) // 2
        odd = i % 2
        off = odd * half + (1 - odd) * (chunks - half)
        c = (my_chunk + off) % chunks

        def add(u, acc):
            return acc + dot(probs[c, u], u_wide[u])

        grad = rounds(c, chunks, add, jnp.zeros((2 * T, W), F32)).astype(BF16)
        lg_out[2 * c] = grad[:T]
        lg_out[2 * c + 1] = grad[T:]
        for side in range(2):

            @pl.when(2 * c + side != me)
            def _():
                mat_copy(1, lg_out, lg_buf, 2 * c + side, me).start()

    rounds(0, chunks, light)
    lg_buf[me] = lg_out[me]

    rounds(1, n, lambda i: mat_copy(0, bs_out, bs_buf, peer_at(i), peer_at(i)).wait_recv())

    def forward(b, carried):
        a, s = carried
        loc_a[0, b] = jnp.broadcast_to(a, (8, W))
        loc_b[0, b] = s
        return absorb(bs_buf.at[b], carried)

    start_rows(0, *rounds(0, n, forward, (one_a, zero_b)))

    rounds(1, n, lambda i: mat_copy(2, mv_out, mv_buf, peer_at(i), peer_at(i)).wait_recv())

    def reach(b):
        reaches[b] = fold(dot(mv_buf[b], lg_out[b]))

    rounds(0, n, reach)

    def backward(j, carried):
        b = n - 1 - j
        a, s = carried
        loc_a[1, b] = jnp.broadcast_to(a, (8, W))
        loc_b[1, b] = s
        total = read_total(bs_buf[b, HD:])
        return a * total, total * s + reaches[b]

    start_rows(1, *rounds(0, n, backward, (one_a, zero_b)))
    part_in = fold_rows(0)
    part_back = fold_rows(1)

    span_in = fold_columns(0, part_in)

    def send_state(i):
        b = peer_at(i)
        st_out[b] = (loc_a[0, b, :1] * span_in + loc_b[0, b]).astype(BF16)

        @pl.when(i > 0)
        def _():
            mat_copy(3, st_out, st_buf, b, me).start()

    rounds(0, n, send_state)
    st_buf[me] = st_out[me]

    span_back = fold_columns(1, part_back)

    def send_reach(i):
        b = peer_at(i)
        ri_out[b] = (loc_a[1, b, :1] * span_back + loc_b[1, b]).astype(BF16)

        @pl.when(i > 0)
        def _():
            mat_copy(4, ri_out, ri_buf, b, me).start()

    rounds(0, n, send_reach)
    ri_buf[me] = ri_out[me]

    def inside(i):
        p = peer_at(i)

        @pl.when(i > 0)
        def _():
            mat_copy(1, lg_out, lg_buf, p, p).wait_recv()

        lg2 = halves(lg_buf[p])
        lk = lk_ref[:, lanes(p)]
        lq = lq_ref[:, lanes(p)]
        back = (dot(lg2, lv_ref[:, lanes(p)], 1, 1) * weights[p]).astype(BF16)
        wide = jnp.concatenate([back[:T], back[T:]], axis=1)
        acc_q[p] = dot(wide, halves(lk))
        acc_k[p] = dot(back, halves(lq), 0, 0)
        acc_v[p] = dot(mixed[p], lg2, 0, 0)

    rounds(0, n, inside)

    def finish_query(i):
        p = peer_at(i)

        @pl.when(i > 0)
        def _():
            mat_copy(3, st_out, st_buf, p, p).wait_recv()

        carried = dot(lg_buf[p], halves(st_buf[p]), 1, 1)
        gq_ref[:, lanes(p)] = (scale * (acc_q[p] + entries[p] * carried)).astype(BF16)

    rounds(0, n, finish_query)

    def finish(i):
        p = peer_at(i)

        @pl.when(i > 0)
        def _():
            mat_copy(4, ri_out, ri_buf, p, p).wait_recv()

        both = halves(ri_buf[p])
        leave = leaving[p]
        from_value = dot(lv_ref[:, lanes(p)], both, 1, 1)
        from_key = dot(lk_ref[:, lanes(p)], both)
        gk_ref[:, lanes(p)] = (scale * (acc_k[p] + leave * from_value)).astype(BF16)
        gv_ref[:, lanes(p)] = (scale * (acc_v[p] + leave * from_key)).astype(BF16)

    rounds(0, n, finish)

    def drain(i):
        p = peer_at(i)
        for which, (src, buf) in enumerate(inputs):
            in_copy(which, src, buf, p, me).wait_send()
        mats = ((bs_out, bs_buf), (lg_out, lg_buf), (mv_out, mv_buf), (st_out, st_buf), (ri_out, ri_buf))
        for which, (src, buf) in enumerate(mats):
            mat_copy(which, src, buf, p, me).wait_send()

    rounds(1, n, drain)
    for which in range(2):
        rounds(1, n_y, lambda i: row_copy(which, (y + i) % n_y, y).wait_send())
        low, high = (0, x) if which else (x + 1, n_x)
        rounds(low, high, lambda k: col_copy(which, k, x).wait_send())


def body(n_ctx, n, *args):
    shape = args[0].shape
    args = (*args[:6], args[6].T, args[7])
    vmem = pl.BlockSpec(memory_space=pltpu.VMEM)
    n_y = 8 if n_ctx % 8 == 0 else 2
    n_x = n_ctx // n_y
    chunks = n // 2
    pairs = (n, T, W)
    mats = (n, HD, W)
    scratch = [
        pltpu.VMEM(pairs, BF16),
        pltpu.VMEM(pairs, BF16),
        pltpu.VMEM(pairs, BF16),
        pltpu.VMEM(pairs, BF16),
        pltpu.VMEM(pairs, BF16),
        pltpu.VMEM((n, MSG, W), BF16),
        pltpu.VMEM((n, MSG, W), BF16),
        pltpu.VMEM(mats, BF16),
        pltpu.VMEM(mats, BF16),
        pltpu.VMEM(pairs, BF16),
        pltpu.VMEM(pairs, BF16),
        pltpu.VMEM(mats, BF16),
        pltpu.VMEM(mats, BF16),
        pltpu.VMEM((2, n_y, MSG, W), BF16),
        pltpu.VMEM((2, MSG, W), BF16),
        pltpu.VMEM((2, n_x, MSG, W), BF16),
        pltpu.VMEM((2, MSG, W), BF16),
        pltpu.VMEM((n, 2 * T, T), F32),
        pltpu.VMEM((2 * n, T), F32),
        pltpu.VMEM((n, T, 2 * T), F32),
        pltpu.VMEM(mats, F32),
        pltpu.VMEM((chunks, 4 * T, W), BF16),
        pltpu.VMEM((n, 2 * T, T), BF16),
        pltpu.VMEM(pairs, F32),
        pltpu.VMEM(pairs, F32),
        pltpu.VMEM((chunks, 2 * T, 4 * T), F32),
        pltpu.VMEM((chunks, chunks, 2 * T, 4 * T), BF16),
        pltpu.VMEM((2, n, 8, W), F32),
        pltpu.VMEM((2, n, HD, W), F32),
        pltpu.VMEM(pairs, F32),
        pltpu.VMEM(pairs, F32),
        pltpu.VMEM(pairs, F32),
        pltpu.SemaphoreType.DMA((3, n)),
        pltpu.SemaphoreType.DMA((3, n)),
        pltpu.SemaphoreType.DMA((5, n)),
        pltpu.SemaphoreType.DMA((5, n)),
        pltpu.SemaphoreType.DMA((2, n_y)),
        pltpu.SemaphoreType.DMA((2, n_y)),
        pltpu.SemaphoreType.DMA((2, n_x)),
        pltpu.SemaphoreType.DMA((2, n_x)),
    ]
    return pl.pallas_call(
        functools.partial(kernel, n_ctx, n_y, n),
        out_shape=[jax.ShapeDtypeStruct(shape, BF16)] * 3,
        in_specs=[vmem] * 7 + [pl.BlockSpec(memory_space=pltpu.SMEM)],
        out_specs=[vmem] * 3,
        scratch_shapes=scratch,
        compiler_params=pltpu.CompilerParams(
            collective_id=0, has_side_effects=True, vmem_limit_bytes=56 * 1024 * 1024
        ),
        name="span_backward",
    )(*args)


def solution(mesh):
    tokens = P(("ctx", "head"), None)
    return jax.shard_map(
        functools.partial(body, mesh.shape["ctx"], mesh.shape["head"]),
        mesh=mesh,
        in_specs=(tokens,) * 7 + (P("ctx", None),),
        out_specs=(tokens,) * 3,
        check_vma=False,
    )
```

time: 130 us -> 107 us (0.82)
  the two profiles are of different devices: /device:TPU:23 before, /device:TPU:1 now
where the time goes in v2:
time: 107 us; the launch traced here: 106 us
  Pallas kernels  102 us (95%)
  local copies, waits for them, and re-layouts  3.97 us (4%)
    pallas_call x1, Pallas kernels, body(): pl.pallas_call(functools.partial(kernel, n_ctx, n_y, n), out_shape=[jax.S...  102 us
    unnamed x7, local copies, waits for them, and re-layouts  3.97 us

profile of v2, /device:TPU:1, one launch (start us, length us, event | category | flops | bytes accessed | tf_op | source)
XLA Modules:
  0.0 106.2 jit_solution(14971634085595701348)
XLA Ops:
  0.6 101.6 %span_backward.1 = (bf16[128,2048]{1,0:T(8,128)(2,1)}, bf16[128,2048]{1,0:T(8,128)(2,1)}, bf16[128,2048]{1,0:T(8,128)(2,1)}) custom-call(bf16[128,2048]{1,0:T(8,128)(2,1)} %lq_ref.1, bf16[128,2048]{1,0:T(8,128)(2,1)} %lk_ref.1, bf16[128,2048]{1,0:T(8,128)(2,1)} %lv_ref.1, bf16[128,2048]{1,0:T(8,128)(2,1)} %sq_ref.1, bf16[128,2048]{1,0:T(8,128)(2,1)} %sk_ref.1, ...), custom_call_target="tpu_custom_call" | custom-call | tf_op jit(solution)/shard_map/span_backward/pallas_call | solution.py:567
  102.2 0.0 copy-start.1
  102.3 1.9 %copy.14 = bf16[128,2048]{1,0:T(8,128)(2,1)} copy(bf16[128,2048]{1,0:T(8,128)(2,1)} %get-tuple-element.6) | data formatting | bytes 1048576
  104.2 0.0 copy-done.1
  104.2 0.0 copy-start
  104.2 0.8 copy.15
  105.0 0.4 copy-done
  105.4 0.8 copy.16
Async XLA Ops:
  102.2 2.0 %copy-start.1 = (bf16[128,2048]{1,0:T(8,128)(2,1)S(1)}, bf16[128,2048]{1,0:T(8,128)(2,1)}, u32[]{:S(2)}) copy-start(bf16[128,2048]{1,0:T(8,128)(2,1)} %get-tuple-element.7) | copy-start | bytes 1572868
  104.2 1.2 %copy-start = (bf16[128,2048]{1,0:T(8,128)(2,1)S(1)}, bf16[128,2048]{1,0:T(8,128)(2,1)}, u32[]{:S(2)}) copy-start(bf16[128,2048]{1,0:T(8,128)(2,1)} %get-tuple-element.8) | copy-start | bytes 1572868

commit v3 on v2

--- a/solution.py
+++ b/solution.py
@@ -49,6 +49,19 @@
     return rows.astype(BF16)
 
 
+def two_totals(first, second):
+    upper, lower = total_rows(first), total_rows(second)
+    return jnp.concatenate([upper[:8].astype(F32), lower[:8].astype(F32)], axis=0).astype(BF16)
+
+
+def read_two(rows):
+    rows = rows.astype(F32)
+    return (
+        jnp.sum(rows[:8], axis=0, keepdims=True),
+        jnp.sum(rows[8:], axis=0, keepdims=True),
+    )
+
+
 def read_total(rows):
     return jnp.sum(rows.astype(F32), axis=0, keepdims=True)
 
@@ -57,9 +70,9 @@
     n_ctx,
     n_y,
     n,
-    lq_ref,
-    lk_ref,
-    lv_ref,
+    lq_hbm,
+    lk_hbm,
+    lv_hbm,
     sq_ref,
     sk_ref,
     up_ref,
@@ -68,13 +81,18 @@
     gq_ref,
     gk_ref,
     gv_ref,
+    lq_ref,
+    lk_ref,
+    lv_ref,
     k_buf,
     q_buf,
     u_buf,
     lg_buf,
     lg_out,
-    bs_buf,
+    bs_mate,
     bs_out,
+    cs_buf,
+    cs_out,
     st_buf,
     st_out,
     mv_buf,
@@ -86,6 +104,7 @@
     col_buf,
     col_out,
     weights,
+    weights_t,
     level_rows,
     level_columns,
     reaches,
@@ -108,13 +127,20 @@
     recv_row,
     send_col,
     recv_col,
+    send_chip,
+    recv_chip,
+    send_mate,
+    recv_mate,
+    local_sem,
 ):
     here = lax.axis_index("ctx")
     me = lax.axis_index("head")
     n_x = n_ctx // n_y
     x, y = here // n_y, here % n_y
     chunks = n // 2
-    scale = 1.0 / (HD * math.sqrt(HD))
+    chips = n // 2
+    chip, core = me // 2, me % 2
+    mate = me + 1 - 2 * core
     root_log2 = math.log2(math.e) / math.sqrt(HD)
 
     def peer_at(i):
@@ -136,6 +162,13 @@
 
         lax.fori_loop(low, high, plain, 0)
 
+    def several(count, step, low=0, high=n):
+        def turn(j):
+            for q in range(count):
+                step(count * j + q)
+
+        rounds(low // count, high // count, turn)
+
     barrier = pltpu.get_barrier_semaphore()
 
     def greet_head(i):
@@ -149,6 +182,13 @@
     rounds(1, n, greet_head)
     rounds(1, n_y, lambda i: greet_ctx(x * n_y + (y + i) % n_y))
     rounds(1, n_x, lambda i: greet_ctx((x + i) % n_x * n_y + y))
+    light = ((lq_hbm, lq_ref), (lk_hbm, lk_ref), (lv_hbm, lv_ref))
+    light_copies = [
+        pltpu.make_async_copy(src, dst, local_sem.at[3 + which])
+        for which, (src, dst) in enumerate(light)
+    ]
+    for copy in light_copies:
+        copy.start()
     pl.semaphore_wait(barrier, n - 1 + n_y - 1 + n_x - 1)
 
     def in_copy(which, src, buf, peer, slot):
@@ -171,6 +211,37 @@
             device_id_type=MESH,
         )
 
+    def chip_copy(which, src, dst, peer, slot):
+        return pltpu.make_async_remote_copy(
+            src_ref=src,
+            dst_ref=dst,
+            send_sem=send_chip.at[which, peer],
+            recv_sem=recv_chip.at[which, slot],
+            device_id=(here, 2 * peer + core),
+            device_id_type=MESH,
+        )
+
+    def sum_copy(peer, slot):
+        return chip_copy(0, cs_out.at[peer], cs_buf.at[slot], peer, slot)
+
+    def state_copy(peer, slot):
+        return chip_copy(1, st_out.at[peer], st_buf.at[core, slot], peer, slot)
+
+    def mate_copy(which, src, dst):
+        return pltpu.make_async_remote_copy(
+            src_ref=src,
+            dst_ref=dst,
+            send_sem=send_mate.at[which],
+            recv_sem=recv_mate.at[which],
+            device_id=(here, mate),
+            device_id_type=MESH,
+        )
+
+    def chip_at(i):
+        half = (i + 1) // 2
+        odd = i % 2
+        return (chip + odd * half + (1 - odd) * (chips - half)) % chips
+
     def row_copy(which, peer, slot):
         return pltpu.make_async_remote_copy(
             src_ref=row_out.at[which],
@@ -237,7 +308,13 @@
     inputs = ((sk_ref, k_buf), (sq_ref, q_buf), (up_ref, u_buf))
     for which, (src, buf) in enumerate(inputs):
         rounds(1, n, lambda i: in_copy(which, src, buf, peer_at(i), me).start())
-        buf[me] = src[:, lanes(me)]
+
+    own_copies = [
+        pltpu.make_async_copy(src.at[:, lanes(me)], buf.at[me], local_sem.at[which])
+        for which, (src, buf) in enumerate(inputs)
+    ]
+    for copy in own_copies:
+        copy.start()
 
     lower = lax.broadcasted_iota(jnp.int32, (T, T), 1) <= lax.broadcasted_iota(
         jnp.int32, (T, T), 0
@@ -257,6 +334,9 @@
 
     for p in range(n):
         level_up(p)
+
+    for copy in light_copies:
+        copy.wait()
 
     def prepare(i):
         p = peer_at(i)
@@ -272,7 +352,9 @@
             ],
             axis=0,
         )
+        table_t = jnp.concatenate([table[:T].T, table[T:].T], axis=1)
         weights[p] = table
+        weights_t[p] = table_t
         first = lax.broadcasted_iota(jnp.int32, (T, W), 1) < HD
         level = jnp.where(first, columns[0], columns[1])
         last = level[T - 1 : T]
@@ -293,16 +375,17 @@
         def _():
             mat_copy(2, mv_out, mv_buf, p, me).start()
 
-        mixed[p] = (dot(halves(lq), lk, 1, 1) * table).astype(BF16)
+        mixed[p] = (dot(lk, halves(lq), 1, 1) * table_t).astype(BF16)
 
     rounds(0, n, prepare)
     mv_buf[me] = mv_out[me]
-    bs_buf[me] = bs_out[me]
-    rounds(1, n, lambda i: mat_copy(0, bs_out, bs_buf, peer_at(i), me).start())
+    sums_to_mate = mate_copy(0, bs_out, bs_mate)
+    sums_to_mate.start()
 
     for which in range(2):
         src, buf = inputs[which]
         rounds(1, n, lambda i: in_copy(which, src, buf, peer_at(i), peer_at(i)).wait_recv())
+        own_copies[which].wait()
 
     def soften(u):
         size = 2 * T
@@ -367,7 +450,29 @@
 
     rounds(0, chunks, soften)
 
+    sums_to_mate.wait_recv()
+
+    def join(i):
+        peer = chip_at(i)
+        p = 2 * peer + core
+        mine, other = bs_out[p, :HD].astype(F32), bs_mate[p, :HD].astype(F32)
+        mine_a, other_a = read_total(bs_out[p, HD:]), read_total(bs_mate[p, HD:])
+        early = jnp.where(core == 0, mine, other)
+        late = jnp.where(core == 0, other, mine)
+        early_a = jnp.where(core == 0, mine_a, other_a)
+        late_a = jnp.where(core == 0, other_a, mine_a)
+        cs_out[peer, :HD] = (late_a * early + late).astype(BF16)
+        cs_out[peer, HD:] = two_totals(early_a, late_a)
+
+        @pl.when(i > 0)
+        def _():
+            sum_copy(peer, chip).start()
+
+    rounds(0, chips, join)
+    cs_buf[chip] = cs_out[chip]
+
     rounds(1, n, lambda i: in_copy(2, up_ref, u_buf, peer_at(i), peer_at(i)).wait_recv())
+    own_copies[2].wait()
 
     def widen(u):
         u_wide[u] = jnp.concatenate([halves(u_buf[2 * u]), halves(u_buf[2 * u + 1])], axis=0)
@@ -376,7 +481,7 @@
 
     my_chunk = me // 2
 
-    def light(i):
+    def light_pair(i):
         half = (i + 1) // 2
         odd = i % 2
         off = odd * half + (1 - odd) * (chunks - half)
@@ -394,51 +499,54 @@
             def _():
                 mat_copy(1, lg_out, lg_buf, 2 * c + side, me).start()
 
-    rounds(0, chunks, light)
+    rounds(0, chunks, light_pair)
     lg_buf[me] = lg_out[me]
-
-    rounds(1, n, lambda i: mat_copy(0, bs_out, bs_buf, peer_at(i), peer_at(i)).wait_recv())
-
-    def forward(b, carried):
-        a, s = carried
-        loc_a[0, b] = jnp.broadcast_to(a, (8, W))
-        loc_b[0, b] = s
-        return absorb(bs_buf.at[b], carried)
-
-    start_rows(0, *rounds(0, n, forward, (one_a, zero_b)))
 
     rounds(1, n, lambda i: mat_copy(2, mv_out, mv_buf, peer_at(i), peer_at(i)).wait_recv())
 
     def reach(b):
         reaches[b] = fold(dot(mv_buf[b], lg_out[b]))
 
-    rounds(0, n, reach)
+    several(4, reach)
+
+    rounds(1, chips, lambda i: sum_copy(chip_at(i), chip_at(i)).wait_recv())
+
+    def forward(c, carried):
+        a, s = carried
+        loc_a[0, c] = jnp.broadcast_to(a, (8, W))
+        loc_b[0, c] = s
+        early_a, late_a = read_two(cs_buf[c, HD:])
+        total = early_a * late_a
+        return a * total, total * s + cs_buf[c, :HD].astype(F32)
+
+    start_rows(0, *rounds(0, chips, forward, (one_a, zero_b)))
 
     def backward(j, carried):
-        b = n - 1 - j
+        c = chips - 1 - j
+        totals = read_two(cs_buf[c, HD:])
         a, s = carried
-        loc_a[1, b] = jnp.broadcast_to(a, (8, W))
-        loc_b[1, b] = s
-        total = read_total(bs_buf[b, HD:])
-        return a * total, total * s + reaches[b]
-
-    start_rows(1, *rounds(0, n, backward, (one_a, zero_b)))
-    part_in = fold_rows(0)
-    part_back = fold_rows(1)
-
-    span_in = fold_columns(0, part_in)
+        for side in (1, 0):
+            loc_a[1, 2 * c + side] = jnp.broadcast_to(a, (8, W))
+            loc_b[1, 2 * c + side] = s
+            a, s = a * totals[side], totals[side] * s + reaches[2 * c + side]
+        return a, s
+
+    start_rows(1, *rounds(0, chips, backward, (one_a, zero_b)))
+
+    span_in = fold_columns(0, fold_rows(0))
 
     def send_state(i):
-        b = peer_at(i)
-        st_out[b] = (loc_a[0, b, :1] * span_in + loc_b[0, b]).astype(BF16)
+        c = chip_at(i)
+        st_out[c] = (loc_a[0, c, :1] * span_in + loc_b[0, c]).astype(BF16)
 
         @pl.when(i > 0)
         def _():
-            mat_copy(3, st_out, st_buf, b, me).start()
-
-    rounds(0, n, send_state)
-    st_buf[me] = st_out[me]
-
+            state_copy(c, chip).start()
+
+    rounds(0, chips, send_state)
+    st_buf[core, chip] = st_out[chip]
+
+    part_back = fold_rows(1)
     span_back = fold_columns(1, part_back)
 
     def send_reach(i):
@@ -452,65 +560,88 @@
     rounds(0, n, send_reach)
     ri_buf[me] = ri_out[me]
 
-    def inside(i):
-        p = peer_at(i)
-
-        @pl.when(i > 0)
-        def _():
-            mat_copy(1, lg_out, lg_buf, p, p).wait_recv()
-
+    rounds(1, n, lambda i: mat_copy(1, lg_out, lg_buf, peer_at(i), peer_at(i)).wait_recv())
+
+    def inside(p):
         lg2 = halves(lg_buf[p])
         lk = lk_ref[:, lanes(p)]
+        lv = lv_ref[:, lanes(p)]
         lq = lq_ref[:, lanes(p)]
-        back = (dot(lg2, lv_ref[:, lanes(p)], 1, 1) * weights[p]).astype(BF16)
+        back = (dot(lg2, lv, 1, 1) * weights[p]).astype(BF16)
+        back_t = (dot(lv, lg2, 1, 1) * weights_t[p]).astype(BF16)
         wide = jnp.concatenate([back[:T], back[T:]], axis=1)
         acc_q[p] = dot(wide, halves(lk))
-        acc_k[p] = dot(back, halves(lq), 0, 0)
-        acc_v[p] = dot(mixed[p], lg2, 0, 0)
-
-    rounds(0, n, inside)
-
-    def finish_query(i):
-        p = peer_at(i)
-
-        @pl.when(i > 0)
-        def _():
-            mat_copy(3, st_out, st_buf, p, p).wait_recv()
-
-        carried = dot(lg_buf[p], halves(st_buf[p]), 1, 1)
-        gq_ref[:, lanes(p)] = (scale * (acc_q[p] + entries[p] * carried)).astype(BF16)
-
-    rounds(0, n, finish_query)
-
-    def finish(i):
-        p = peer_at(i)
-
-        @pl.when(i > 0)
-        def _():
-            mat_copy(4, ri_out, ri_buf, p, p).wait_recv()
-
+        acc_k[p] = dot(back_t, halves(lq))
+        acc_v[p] = dot(mixed[p], lg2)
+
+    several(2, inside, 0, n // 2)
+
+    rounds(1, chips, lambda i: state_copy(chip_at(i), chip_at(i)).wait_recv())
+    states_to_mate = mate_copy(1, st_buf.at[core], st_buf.at[core])
+    states_to_mate.start()
+
+    several(2, inside, n // 2, n)
+    states_to_mate.wait_recv()
+
+    def finish_query(p):
+        state = st_buf[p % 2, p // 2].astype(F32)
+        passed = read_total(bs_mate[p, HD:]) * state + bs_mate[p, :HD].astype(F32)
+        state = jnp.where(core == 1, passed, state)
+        high = state.astype(BF16)
+        low = (state - high.astype(F32)).astype(BF16)
+        lg = lg_buf[p]
+        carried = dot(lg, halves(high), 1, 1) + dot(lg, halves(low), 1, 1)
+        gq_ref[:, lanes(p)] = (acc_q[p] + entries[p] * carried).astype(BF16)
+
+    several(2, finish_query)
+
+    def finish(p):
         both = halves(ri_buf[p])
         leave = leaving[p]
         from_value = dot(lv_ref[:, lanes(p)], both, 1, 1)
         from_key = dot(lk_ref[:, lanes(p)], both)
-        gk_ref[:, lanes(p)] = (scale * (acc_k[p] + leave * from_value)).astype(BF16)
-        gv_ref[:, lanes(p)] = (scale * (acc_v[p] + leave * from_key)).astype(BF16)
-
-    rounds(0, n, finish)
+        gk_ref[:, lanes(p)] = (acc_k[p] + leave * from_value).astype(BF16)
+        gv_ref[:, lanes(p)] = (acc_v[p] + leave * from_key).astype(BF16)
+
+    def finish_two(j):
+        first, second = peer_at(2 * j), peer_at(2 * j + 1)
+
+        @pl.when(j > 0)
+        def _():
+            mat_copy(4, ri_out, ri_buf, first, first).wait_recv()
+
+        mat_copy(4, ri_out, ri_buf, second, second).wait_recv()
+        finish(first)
+        finish(second)
+
+    rounds(0, n // 2, finish_two)
 
     def drain(i):
         p = peer_at(i)
         for which, (src, buf) in enumerate(inputs):
             in_copy(which, src, buf, p, me).wait_send()
-        mats = ((bs_out, bs_buf), (lg_out, lg_buf), (mv_out, mv_buf), (st_out, st_buf), (ri_out, ri_buf))
-        for which, (src, buf) in enumerate(mats):
+        for which, src, buf in ((1, lg_out, lg_buf), (2, mv_out, mv_buf), (4, ri_out, ri_buf)):
             mat_copy(which, src, buf, p, me).wait_send()
 
     rounds(1, n, drain)
+
+    def drain_chip(i):
+        sum_copy(chip_at(i), chip).wait_send()
+        state_copy(chip_at(i), chip).wait_send()
+
+    rounds(1, chips, drain_chip)
+    sums_to_mate.wait_send()
+    states_to_mate.wait_send()
     for which in range(2):
         rounds(1, n_y, lambda i: row_copy(which, (y + i) % n_y, y).wait_send())
         low, high = (0, x) if which else (x + 1, n_x)
         rounds(low, high, lambda k: col_copy(which, k, x).wait_send())
+
+
+def scale_kernel(*refs):
+    scale = 1.0 / (HD * math.sqrt(HD))
+    for src, dst in zip(refs[:3], refs[3:]):
+        dst[...] = (src[...].astype(F32) * scale).astype(BF16)
 
 
 def body(n_ctx, n, *args):
@@ -523,6 +654,9 @@
     pairs = (n, T, W)
     mats = (n, HD, W)
     scratch = [
+        pltpu.VMEM(shape, BF16),
+        pltpu.VMEM(shape, BF16),
+        pltpu.VMEM(shape, BF16),
         pltpu.VMEM(pairs, BF16),
         pltpu.VMEM(pairs, BF16),
         pltpu.VMEM(pairs, BF16),
@@ -530,8 +664,10 @@
         pltpu.VMEM(pairs, BF16),
         pltpu.VMEM((n, MSG, W), BF16),
         pltpu.VMEM((n, MSG, W), BF16),
-        pltpu.VMEM(mats, BF16),
-        pltpu.VMEM(mats, BF16),
+        pltpu.VMEM((chunks, MSG, W), BF16),
+        pltpu.VMEM((chunks, MSG, W), BF16),
+        pltpu.VMEM((2, chunks, HD, W), BF16),
+        pltpu.VMEM((chunks, HD, W), BF16),
         pltpu.VMEM(pairs, BF16),
         pltpu.VMEM(pairs, BF16),
         pltpu.VMEM(mats, BF16),
@@ -541,11 +677,12 @@
         pltpu.VMEM((2, n_x, MSG, W), BF16),
         pltpu.VMEM((2, MSG, W), BF16),
         pltpu.VMEM((n, 2 * T, T), F32),
+        pltpu.VMEM((n, T, 2 * T), F32),
         pltpu.VMEM((2 * n, T), F32),
         pltpu.VMEM((n, T, 2 * T), F32),
         pltpu.VMEM(mats, F32),
         pltpu.VMEM((chunks, 4 * T, W), BF16),
-        pltpu.VMEM((n, 2 * T, T), BF16),
+        pltpu.VMEM((n, T, 2 * T), BF16),
         pltpu.VMEM(pairs, F32),
         pltpu.VMEM(pairs, F32),
         pltpu.VMEM((chunks, 2 * T, 4 * T), F32),
@@ -563,11 +700,16 @@
         pltpu.SemaphoreType.DMA((2, n_y)),
         pltpu.SemaphoreType.DMA((2, n_x)),
         pltpu.SemaphoreType.DMA((2, n_x)),
+        pltpu.SemaphoreType.DMA((2, chunks)),
+        pltpu.SemaphoreType.DMA((2, chunks)),
+        pltpu.SemaphoreType.DMA((2,)),
+        pltpu.SemaphoreType.DMA((2,)),
+        pltpu.SemaphoreType.DMA((6,)),
     ]
-    return pl.pallas_call(
+    sums = pl.pallas_call(
         functools.partial(kernel, n_ctx, n_y, n),
         out_shape=[jax.ShapeDtypeStruct(shape, BF16)] * 3,
-        in_specs=[vmem] * 7 + [pl.BlockSpec(memory_space=pltpu.SMEM)],
+        in_specs=[pl.BlockSpec(memory_space=pl.ANY)] * 6 + [vmem] + [pl.BlockSpec(memory_space=pltpu.SMEM)],
         out_specs=[vmem] * 3,
         scratch_shapes=scratch,
         compiler_params=pltpu.CompilerParams(
@@ -575,6 +717,13 @@
         ),
         name="span_backward",
     )(*args)
+    return pl.pallas_call(
+        scale_kernel,
+        out_shape=[jax.ShapeDtypeStruct(shape, BF16)] * 3,
+        in_specs=[vmem] * 3,
+        out_specs=[vmem] * 3,
+        name="scale_gradients",
+    )(*sums)
 
 
 def solution(mesh):

time: 107 us -> 100 us (0.935)
  local copies, waits for them, and re-layouts: 3.97 us -> 0 us
  Pallas kernels: 102 us -> 99.2 us
    pallas_call x1, Pallas kernels: 102 us -> 96.7 us  [body(): pl.pallas_call(functools.partial(kernel, n_ctx, n_y, n), out_shape=[jax.S...]
    unnamed x7 -> x0, local copies, waits for them, and re-layouts: 3.97 us -> none
    pallas_call x0 -> x1, Pallas kernels: none -> 2.58 us  [body(): pl.pallas_call(scale_kernel, out_shape=[jax.ShapeDtypeStruct(shape, BF16)...]
where the time goes in v3:
time: 100 us; the launch traced here: 99.9 us
  Pallas kernels  99.2 us (99%)
    pallas_call x1, Pallas kernels, body(): pl.pallas_call(functools.partial(kernel, n_ctx, n_y, n), out_shape=[jax.S...  96.7 us
    pallas_call x1, Pallas kernels, body(): pl.pallas_call(scale_kernel, out_shape=[jax.ShapeDtypeStruct(shape, BF16)...  2.58 us

profile of v3, /device:TPU:1, one launch (start us, length us, event | category | flops | bytes accessed | tf_op | source)
XLA Modules:
  0.0 99.9 jit_solution(1471172862964854470)
XLA Ops:
  0.6 96.7 %span_backward.1 = (bf16[128,2048]{1,0:T(8,128)(2,1)}, bf16[128,2048]{1,0:T(8,128)(2,1)}, bf16[128,2048]{1,0:T(8,128)(2,1)}) custom-call(bf16[128,2048]{1,0:T(8,128)(2,1)} %lq_hbm.1, bf16[128,2048]{1,0:T(8,128)(2,1)} %lk_hbm.1, bf16[128,2048]{1,0:T(8,128)(2,1)} %lv_hbm.1, bf16[128,2048]{1,0:T(8,128)(2,1)} %sq_ref.1, bf16[128,2048]{1,0:T(8,128)(2,1)} %sk_ref.1, ...), custom_call_target="tpu_custom_call" | custom-call | tf_op jit(solution)/shard_map/span_backward/pallas_call | solution.py:709
  97.3 2.6 %scale_gradients.1 = (bf16[128,2048]{1,0:T(8,128)(2,1)}, bf16[128,2048]{1,0:T(8,128)(2,1)}, bf16[128,2048]{1,0:T(8,128)(2,1)}) custom-call(bf16[128,2048]{1,0:T(8,128)(2,1)} %get-tuple-element.6.refs_0_, bf16[128,2048]{1,0:T(8,128)(2,1)} %get-tuple-element.7.refs_1_, bf16[128,2048]{1,0:T(8,128)(2,1)} %get-tuple-element.8.refs_2_), custom_call_target="tpu_custom_call" | custom-call | tf_op jit(solution)/shard_map/scale_gradients/pallas_call | solution.py:720

commit v4 on v3

--- a/solution.py
+++ b/solution.py
@@ -533,7 +533,9 @@
 
     start_rows(1, *rounds(0, chips, backward, (one_a, zero_b)))
 
-    span_in = fold_columns(0, fold_rows(0))
+    part_in = fold_rows(0)
+    part_back = fold_rows(1)
+    span_in = fold_columns(0, part_in)
 
     def send_state(i):
         c = chip_at(i)
@@ -546,7 +548,6 @@
     rounds(0, chips, send_state)
     st_buf[core, chip] = st_out[chip]
 
-    part_back = fold_rows(1)
     span_back = fold_columns(1, part_back)
 
     def send_reach(i):
@@ -557,7 +558,7 @@
         def _():
             mat_copy(4, ri_out, ri_buf, b, me).start()
 
-    rounds(0, n, send_reach)
+    several(2, send_reach)
     ri_buf[me] = ri_out[me]
 
     rounds(1, n, lambda i: mat_copy(1, lg_out, lg_buf, peer_at(i), peer_at(i)).wait_recv())
@@ -706,6 +707,7 @@
         pltpu.SemaphoreType.DMA((2,)),
         pltpu.SemaphoreType.DMA((6,)),
     ]
+    rows = pl.BlockSpec((shape[0] // 4, shape[1]), lambda i: (i, 0))
     sums = pl.pallas_call(
         functools.partial(kernel, n_ctx, n_y, n),
         out_shape=[jax.ShapeDtypeStruct(shape, BF16)] * 3,
@@ -720,8 +722,9 @@
     return pl.pallas_call(
         scale_kernel,
         out_shape=[jax.ShapeDtypeStruct(shape, BF16)] * 3,
-        in_specs=[vmem] * 3,
-        out_specs=[vmem] * 3,
+        grid=(4,),
+        in_specs=[rows] * 3,
+        out_specs=[rows] * 3,
         name="scale_gradients",
     )(*sums)
 

time: 100 us -> 98.9 us (0.989)
  Pallas kernels: 99.2 us -> 98 us
    pallas_call x1, Pallas kernels: 96.7 us -> 94.4 us  [body(): pl.pallas_call(functools.partial(kernel, n_ctx, n_y, n), out_shape=[jax.S...]
    pallas_call x1, Pallas kernels: 2.58 us -> 3.62 us  [body(): pl.pallas_call(scale_kernel, out_shape=[jax.ShapeDtypeStruct(shape, BF16)...]
where the time goes in v4:
time: 98.9 us; the launch traced here: 98.7 us
  Pallas kernels  98 us (99%)
    pallas_call x1, Pallas kernels, body(): pl.pallas_call(functools.partial(kernel, n_ctx, n_y, n), out_shape=[jax.S...  94.4 us
    pallas_call x1, Pallas kernels, body(): pl.pallas_call(scale_kernel, out_shape=[jax.ShapeDtypeStruct(shape, BF16)...  3.62 us

profile of v4, /device:TPU:1, one launch (start us, length us, event | category | flops | bytes accessed | tf_op | source)
XLA Modules:
  0.0 98.7 jit_solution(1860903760478339508)
XLA Ops:
  0.6 94.4 %span_backward.1 = (bf16[128,2048]{1,0:T(8,128)(2,1)}, bf16[128,2048]{1,0:T(8,128)(2,1)}, bf16[128,2048]{1,0:T(8,128)(2,1)}) custom-call(bf16[128,2048]{1,0:T(8,128)(2,1)} %lq_hbm.1, bf16[128,2048]{1,0:T(8,128)(2,1)} %lk_hbm.1, bf16[128,2048]{1,0:T(8,128)(2,1)} %lv_hbm.1, bf16[128,2048]{1,0:T(8,128)(2,1)} %sq_ref.1, bf16[128,2048]{1,0:T(8,128)(2,1)} %sk_ref.1, ...), custom_call_target="tpu_custom_call" | custom-call | tf_op jit(solution)/shard_map/span_backward/pallas_call | solution.py:711
  95.0 3.6 %scale_gradients.1 = (bf16[128,2048]{1,0:T(8,128)(2,1)}, bf16[128,2048]{1,0:T(8,128)(2,1)}, bf16[128,2048]{1,0:T(8,128)(2,1)}) custom-call(bf16[128,2048]{1,0:T(8,128)(2,1)} %get-tuple-element.6.refs_0_, bf16[128,2048]{1,0:T(8,128)(2,1)} %get-tuple-element.7.refs_1_, bf16[128,2048]{1,0:T(8,128)(2,1)} %get-tuple-element.8.refs_2_), custom_call_target="tpu_custom_call" | custom-call | tf_op jit(solution)/shard_map/scale_gradients/pallas_call | solution.py:722
